TPU v7x, 32 devices: a whole 2x2x4 slice. The times are simulated.
32 devices in a mesh: seq: 4 (over y, x), tensor: 8 (over z, core).
Axes of the slice: x: 2, y: 2, z: 4, core: 2. Of those that a mesh axis runs over, the one named last changes fastest.
Arguments:
- tokens: bfloat16 [4096, 4096], P(('seq', 'tensor')), may hold values from -36 to 36
- norm_gain: float32 [4096], replicated, may hold values from 0.1 to 1.9
- in_weight: bfloat16 [4096, 3, 4096], P(None, None, 'tensor'), may hold values from -0.09375 to 0.09375
- short_filter: float32 [3, 3, 4096], P(None, None, 'tensor'), may hold values from -3 to 3
- filter_spectrum: float32 [2, 8, 4096, 1024], P(None, 'seq', 'tensor'), may hold values from -4 to 4
- out_weight: bfloat16 [4096, 4096], P('tensor'), may hold values from -0.09375 to 0.09375
Outputs:
- mixer_out: bfloat16 [4096, 4096], P(('seq', 'tensor'))
All inputs are finite; a program needn't handle non-finite values.
Results may differ from a plain program's by a relative error of at most 0.012.
Values may be sent and summed in bfloat16 or wider, within the bound.
A program may use at most 192 MiB of HBM per device.

v0:
```python
import math

import jax
import jax.numpy as jnp
from jax import lax
from jax.sharding import PartitionSpec as P

MONARCH = 32
TAPS = 3


EPS = 1e-06
TABLE_PRECISION = lax.Precision.HIGH
FULL_TURN = 2.0 * math.pi


def shifted(block, axis, distance):
    devices = range(lax.axis_size(axis))
    route = [(i - distance, i) for i in devices if i - distance in devices]
    return lax.ppermute(block, axis, route)


def as_sent(value):
    return jax.tree.map(lambda a: a.astype(jnp.bfloat16) if a.dtype == jnp.float32 else a, value)


def turn_table(count, orient):
    index = jnp.arange(count, dtype=jnp.int32)
    angle = FULL_TURN * (index[:, None] * index[None, :] % count).astype(jnp.float32) / count
    return (jnp.cos(angle), orient * jnp.sin(angle))


def twist(real_part, imag_part, table_cos, table_sin, form):
    cos_real = jnp.einsum(form, table_cos, real_part, precision=TABLE_PRECISION)
    sin_real = jnp.einsum(form, table_sin, real_part, precision=TABLE_PRECISION)
    cos_imag = jnp.einsum(form, table_cos, imag_part, precision=TABLE_PRECISION)
    sin_imag = jnp.einsum(form, table_sin, imag_part, precision=TABLE_PRECISION)
    return (cos_real - sin_imag, cos_imag + sin_real)


def local_dft(real_part, imag_part, orient):
    length = real_part.shape[-1]
    first = MONARCH
    second = length // first
    leading = real_part.shape[:-1]
    real_part = real_part.reshape(leading + (first, second))
    imag_part = imag_part.reshape(leading + (first, second))
    cos_first, sin_first = turn_table(first, orient)
    real_part, imag_part = twist(real_part, imag_part, cos_first, sin_first, "ca,...ab->...cb")
    outer_index = jnp.arange(first, dtype=jnp.int32)[:, None]
    inner_index = jnp.arange(second, dtype=jnp.int32)[None, :]
    angle = FULL_TURN * (outer_index * inner_index % length).astype(jnp.float32) / length
    cos_middle = jnp.cos(angle)
    sin_middle = orient * jnp.sin(angle)
    real_part, imag_part = (
        real_part * cos_middle - imag_part * sin_middle,
        imag_part * cos_middle + real_part * sin_middle,
    )
    cos_second, sin_second = turn_table(second, orient)
    real_part, imag_part = twist(real_part, imag_part, cos_second, sin_second, "db,...cb->...dc")
    return (real_part.reshape(leading + (length,)), imag_part.reshape(leading + (length,)))


def rotate(real_part, imag_part, freq_index, row_index, total_length, orient):
    angle = (
        FULL_TURN
        * (freq_index[:, None] * row_index[None, :] % total_length).astype(jnp.float32)
        / total_length
    )
    cos_turn = jnp.cos(angle)[:, None, :]
    sin_turn = orient * jnp.sin(angle)[:, None, :]
    return (
        real_part * cos_turn - imag_part * sin_turn,
        imag_part * cos_turn + real_part * sin_turn,
    )


def block_dft(blocks, row_index, total_length):
    count = blocks.shape[0]
    freq_count = 2 * count
    freq_index = jnp.arange(freq_count, dtype=jnp.int32)
    block_index = jnp.arange(count, dtype=jnp.int32)
    angle = (
        FULL_TURN
        * (freq_index[:, None] * block_index[None, :] % freq_count).astype(jnp.float32)
        / freq_count
    )
    real_part = jnp.einsum("ks,scr->kcr", jnp.cos(angle), blocks, precision=TABLE_PRECISION)
    imag_part = -jnp.einsum("ks,scr->kcr", jnp.sin(angle), blocks, precision=TABLE_PRECISION)
    real_part, imag_part = rotate(real_part, imag_part, freq_index, row_index, total_length, -1.0)
    return jnp.stack([real_part, imag_part])


def block_idft(real_part, imag_part, total_length):
    freq_count = real_part.shape[0]
    count = freq_count // 2
    block_index = jnp.arange(count, dtype=jnp.int32)
    freq_index = jnp.arange(freq_count, dtype=jnp.int32)
    angle = (
        FULL_TURN
        * (block_index[:, None] * freq_index[None, :] % freq_count).astype(jnp.float32)
        / freq_count
    )
    value = jnp.einsum("sk,kcr->scr", jnp.cos(angle), real_part, precision=TABLE_PRECISION)
    value = value - jnp.einsum("sk,kcr->scr", jnp.sin(angle), imag_part, precision=TABLE_PRECISION)
    return value / total_length


def apply_filter(frequency, filter_part):
    real_part, imag_part = local_dft(frequency[0], frequency[1], -1.0)
    filter_real = filter_part[0]
    filter_imag = filter_part[1]
    product_real = real_part * filter_real - imag_part * filter_imag
    product_imag = real_part * filter_imag + imag_part * filter_real
    return local_dft(product_real, product_imag, 1.0)


def per_device(tokens, norm_gain, in_weight, short_filter, filter_spectrum, out_weight):
    seq_count = lax.axis_size("seq")
    seq_place = lax.axis_index("seq")
    inputs = tokens.astype(jnp.float32)
    square_mean = jnp.mean(inputs * inputs, axis=-1, keepdims=True)
    normed = (inputs / jnp.sqrt(square_mean + EPS) * norm_gain).astype(jnp.bfloat16)
    model_width = in_weight.shape[0]
    width = in_weight.shape[2]
    flat_weight = in_weight.reshape(model_width, 3 * width)
    projected = jnp.dot(
        lax.all_gather(normed, "tensor", axis=0, tiled=True),
        flat_weight,
        preferred_element_type=jnp.float32,
    ).astype(jnp.bfloat16)
    rows = projected.shape[0]
    carried = shifted(projected[rows - (TAPS - 1) :], "seq", 1)
    extended = (
        jnp.concatenate([carried, projected], axis=0)
        .astype(jnp.float32)
        .reshape(rows + TAPS - 1, 3, width)
    )
    short = jnp.zeros((rows, 3, width), jnp.float32)
    for offset in range(TAPS):
        short = (
            short + short_filter[offset] * extended[TAPS - 1 - offset : TAPS - 1 - offset + rows]
        )
    queries = short[:, 0]
    product_cols = (short[:, 1] * short[:, 2]).astype(jnp.bfloat16).T
    total_length = 2 * rows * seq_count
    all_rows = jnp.arange(rows, dtype=jnp.int32)
    piece_rows = rows // seq_count
    gathered = lax.all_to_all(
        product_cols.reshape(1, width, rows), "seq", split_axis=2, concat_axis=0, tiled=True
    )
    own_rows = seq_place * piece_rows + jnp.arange(piece_rows, dtype=jnp.int32)
    partial_spec = block_dft(gathered.astype(jnp.float32), own_rows, total_length)
    frequency = lax.all_to_all(
        partial_spec.astype(jnp.bfloat16), "seq", split_axis=1, concat_axis=3, tiled=True
    ).astype(partial_spec.dtype)
    real_part, imag_part = apply_filter(frequency, filter_spectrum)
    own_freq = 2 * seq_place + jnp.arange(2, dtype=jnp.int32)
    real_part, imag_part = rotate(real_part, imag_part, own_freq, all_rows, total_length, 1.0)
    returned = lax.all_to_all(
        jnp.stack([real_part, imag_part]).astype(jnp.bfloat16),
        "seq",
        split_axis=3,
        concat_axis=1,
        tiled=True,
    ).astype(jnp.float32)
    value_blocks = block_idft(returned[0], returned[1], total_length)
    value_cols = lax.all_to_all(
        as_sent(value_blocks), "seq", split_axis=0, concat_axis=2, tiled=True
    ).astype(value_blocks.dtype)
    long_conv = value_cols[0].T
    gated = (queries * long_conv).astype(jnp.bfloat16)
    summed = lax.psum_scatter(
        jnp.dot(gated, out_weight, preferred_element_type=jnp.float32).astype(jnp.bfloat16),
        "tensor",
        scatter_dimension=0,
        tiled=True,
    ).astype(jnp.float32)
    return (inputs + summed).astype(jnp.bfloat16)


def solution(mesh):
    in_specs = (
        P(("seq", "tensor"), None),
        P(),
        P(None, None, "tensor"),
        P(None, None, "tensor"),
        P(None, "seq", "tensor", None),
        P("tensor", None),
    )
    out_specs = P(("seq", "tensor"), None)
    return jax.shard_map(
        per_device, mesh=mesh, in_specs=in_specs, out_specs=out_specs, check_vma=False
    )
```

profile of v0, /device:TPU:8, one launch (start us, length us, event | category | flops | bytes accessed | tf_op | source)
XLA Modules:
  0.0 545.5 jit_solution(9565816952888031319)
XLA Ops:
  6.5 1.5 fusion.36
  8.1 2.5 fusion.38
  10.6 16.9 %copy.89 = bf16[4096,3,512]{0,2,1:T(8,128)(2,1)} copy(bf16[4096,3,512]{2,0,1:T(8,128)(2,1)} %param.8) | data formatting | bytes 25165824 | tf_op args[2]
  27.5 63.9 %all-gather.2.cloned.1.call-done = bf16[1024,4096]{1,0:T(8,128)(2,1)} async-done(((bf16[128,4096]{1,0:T(8,128)(2,1)}), bf16[1024,4096]{1,0:T(8,128)(2,1)}) %all-gather.2.cloned.1.call-update) | async-done | bytes 8388624 | tf_op jit(solution)/shard_map/all_gather | solution.py:128
  91.4 18.3 %convolution_convert_fusion.1 = bf16[1024,1536]{1,0:T(8,128)(2,1)S(1)} fusion(bf16[1024,4096]{1,0:T(8,128)(2,1)} %all-gather.2.cloned.1.call-done, bf16[4096,1536]{0,1:T(8,128)(2,1)} %bitcast.210), kind=kOutput, calls=%fused_computation.50 | convolution fusion | flops 12886474752 | bytes 24117248 | tf_op jit(solution)/shard_map/dot_general | solution.py:127
  109.7 3.6 collective-permute-start
  113.3 1.3 collective-permute-done
  114.6 1.0 maximum_convert_fusion
  115.5 7.2 %fusion.229 = (f32[1024,1536]{1,0:T(8,128)}, f32[1024,1536]{1,0:T(8,128)}, f32[1024,1536]{1,0:T(8,128)}) fusion(f32[1026,1536]{1,0:T(8,128)S(1)} %maximum_convert_fusion), kind=kLoop, calls=%fused_computation.263 | loop fusion | bytes 37748736 | tf_op jit(solution)/shard_map/slice | solution.py:142
  122.7 6.6 %copy.90 = f32[1024,1536]{0,1:T(8,128)} copy(f32[1024,1536]{1,0:T(8,128)} %get-tuple-element.17) | data formatting | bytes 12582912 | tf_op jit(solution)/shard_map/slice | solution.py:142
  129.3 6.6 %copy.91 = f32[1024,1536]{0,1:T(8,128)} copy(f32[1024,1536]{1,0:T(8,128)} %get-tuple-element.19) | data formatting | bytes 12582912 | tf_op jit(solution)/shard_map/slice | solution.py:142
  135.8 6.6 %copy.92 = f32[1024,1536]{0,1:T(8,128)} copy(f32[1024,1536]{1,0:T(8,128)} %get-tuple-element.18) | data formatting | bytes 12582912 | tf_op jit(solution)/shard_map/slice | solution.py:142
  142.4 7.1 %multiply_add_fusion = f32[1024,3,512]{0,2,1:T(8,128)S(1)} fusion(f32[1024,3,512]{0,2,1:T(8,128)} %bitcast.203, f32[1024,3,512]{0,2,1:T(8,128)} %bitcast.202, f32[1024,3,512]{0,2,1:T(8,128)} %bitcast.201, f32[3,512]{1,0:T(4,128)S(1)} %get-tuple-element.25, f32[3,512]{1,0:T(4,128)S(1)} %get-tuple-element.26, f32[3,512]{1,0:T(4,128)S(1)} %get-tuple-element.24), kind=kLoop, calls=%fused_computation.1 | loop fusion | flops 7864320 | bytes 25184256 | tf_op jit(solution)/shard_map/add | solution.py:142
  149.6 2.7 copy-done.1
  153.1 1.6 copy.178
  155.3 7.0 %reduce = bf16[1024,512]{1,0:T(8,128)(2,1)S(1)} reduce(bf16[1024,1,512]{2,1,0:T(2,128)(2,1)S(1)} %bitcast.212, bf16[]{:T(256)} %broadcast.422), dimensions={1}, to_apply=%bitcast.198.reduce_sub_computation | reduce | bytes 2097154
  162.3 2.0 reshape.261
  164.3 5.0 all-to-all-start
  169.4 13.5 %all-to-all-done = bf16[4,2,65536]{2,1,0:T(2,128)(2,1)S(1)} async-done(((bf16[4,2,65536]{2,1,0:T(2,128)(2,1)}), bf16[4,2,65536]{2,1,0:T(2,128)(2,1)S(1)}, u32[]{:S(2)}, u32[]{:S(2)}) %all-to-all-start) | async-done | bytes 1048608 | tf_op jit(solution)/shard_map/all_to_all | solution.py:149
  184.9 1.6 fusion.52
  186.5 3.0 fusion.40
  189.9 2.9 copy.96
  192.8 4.9 all-to-all-start.1
  198.0 8.5 %fusion.228 = (f32[1,2,512,1024]{3,2,1,0:T(8,128)}, f32[1,2,512,1024]{3,2,1,0:T(8,128)}) fusion(f32[2,2,512,1024]{3,2,1,0:T(8,128)} %param.10), kind=kLoop, calls=%fused_computation.262 | loop fusion | bytes 16777216 | tf_op jit(solution)/shard_map/slice | solution.py:111
  206.5 5.4 copy.134
  211.9 5.4 copy.135
  217.7 27.7 %all-to-all-done.1 = bf16[2,8,512,256]{3,2,0,1:T(8,128)(2,1)} async-done(((bf16[2,8,512,256]{3,2,0,1:T(8,128)(2,1)}), bf16[2,8,512,256]{3,2,0,1:T(8,128)(2,1)}, u32[]{:S(2)}, u32[]{:S(2)}) %all-to-all-start.1) | async-done | bytes 4194336 | tf_op jit(solution)/shard_map/all_to_all | solution.py:154
  245.4 2.5 copy.97
  247.8 2.3 fusion.231
  250.1 2.8 copy.98
  253.0 4.3 fusion.49
  257.3 4.3 copy.100
  261.6 3.9 fusion.45
  265.6 2.7 convolution_subtract_fusion.1
  268.3 3.8 fusion.8
  272.2 5.0 fusion.20
  277.2 6.7 %fusion.18 = f32[2,512,32,32]{1,3,2,0:T(8,128)} fusion(f32[2,512,32,32]{1,2,3,0:T(8,128)S(1)} %get-tuple-element.10), kind=kOutput, calls=%fused_computation.42 | convolution fusion | flops 201340928 | bytes 8388608 | tf_op jit(solution)/shard_map/db,...cb->...dc/dot_general | solution.py:36
  283.8 5.1 fusion.26
  288.9 11.5 %fusion.6 = (f32[2,512,32,32]{1,2,3,0:T(8,128)S(1)}, f32[2,512,32,32]{1,2,3,0:T(8,128)S(1)}) fusion(f32[2,512,32,32]{1,3,2,0:T(8,128)S(1)} %fusion.26, f32[2,512,32,32]{1,3,2,0:T(8,128)} %bitcast.207, f32[2,512,32,32]{1,3,2,0:T(8,128)S(1)} %bitcast.206, f32[2,512,32,32]{1,3,2,0:T(8,128)} %fusion.18, f32[2,512,32,32]{1,2,3,0:T(8,128)S(1)} %get-tuple-element.9), kind=kOutput, calls=%fused_computation.20 | convolution fusion | flops 208681984 | bytes 29360128 | tf_op jit(solution)/shard_map/db,...cb->...dc/dot_general | solution.py:35
  300.4 2.4 fusion.72
  302.8 2.4 fusion.70
  305.1 2.7 convolution_subtract_fusion
  307.9 4.0 fusion.4
  311.8 4.9 fusion.12
  316.7 4.7 fusion.10
  321.4 5.1 subtract_bitcast_fusion
  326.5 2.8 copy.119
  329.4 5.1 add_bitcast_fusion
  334.5 2.4 copy.122
  336.9 1.9 fusion.1
  339.2 6.3 %copy.123 = bf16[2,2,512,1024]{2,1,0,3:T(2,128)(2,1)} copy(bf16[2,2,512,1024]{2,3,1,0:T(8,128)(2,1)S(1)} %pad_maximum_fusion.1) | data formatting | bytes 8388608 | tf_op jit(solution)/shard_map/stack | solution.py:161
  345.5 51.1 %all_to_all.57 = bf16[2,2,512,1024]{2,1,0,3:T(2,128)(2,1)S(1)} all-to-all(bf16[2,2,512,1024]{2,1,0,3:T(2,128)(2,1)} %copy.123), channel_id=1, replica_groups=mesh['seq'=4,'tensor'=8] {'seq'}, dimensions={3} | all-to-all | bytes 8388608 | tf_op jit(solution)/shard_map/all_to_all | solution.py:160
  397.4 2.4 fusion.230
  399.8 5.0 copy.125
  404.8 2.2 squeeze.21
  407.1 2.9 fusion.134
  409.9 6.3 %copy.126 = bf16[1,4,2,512,256]{4,2,1,3,0:T(2,128)(2,1)} copy(bf16[1,4,2,512,256]{3,4,1,2,0:T(8,128)(2,1)} %get-tuple-element.20) | data formatting | bytes 4194304 | tf_op jit(solution)/shard_map/slice | solution.py:167
  416.2 4.1 squeeze.22
  420.4 3.1 multiply_convert_fusion
  423.7 14.8 %all_to_all.58 = bf16[4,512,256]{2,1,0:T(8,128)(2,1)S(1)} all-to-all(bf16[4,512,256]{2,1,0:T(8,128)(2,1)S(1)} %copy.127), channel_id=1, replica_groups=mesh['seq'=4,'tensor'=8] {'seq'}, dimensions={0} | all-to-all | bytes 2097152 | tf_op jit(solution)/shard_map/all_to_all | solution.py:168
  438.7 1.4 copy.128
  440.9 8.6 %convolution_convert_fusion = bf16[1024,4096]{1,0:T(8,128)(2,1)} fusion(bf16[512,4096]{1,0:T(8,128)(2,1)S(1)} %copy-done.6, f32[1024,3,512]{0,2,1:T(8,128)} %copy-done.1, f32[512,1024]{1,0:T(8,128)S(1)} %bitcast.216), kind=kOutput, calls=%fused_computation | convolution fusion | flops 4300210176 | bytes 16777216 | tf_op jit(solution)/shard_map/dot_general | solution.py:174
  449.5 86.4 %reduce-scatter.2.cloned.1.call-done = bf16[128,4096]{1,0:T(8,128)(2,1)} async-done(((bf16[1024,4096]{1,0:T(8,128)(2,1)}), bf16[128,4096]{1,0:T(8,128)(2,1)}) %reduce-scatter.2.cloned.1.call-update) | async-done | bytes 1048592 | tf_op jit(solution)/shard_map/reduce_scatter | solution.py:173
  536.0 2.4 fusion.39
  (42 shorter events, 6.9 us)
Async XLA Ops:
  6.5 84.8 %all-gather.2.cloned.1.call-start = ((), (), s32[]{:S(2)}) async-start(), calls=%async_computation.5 | async-start | bytes 9437184 | tf_op jit(solution)/shard_map/all_gather | solution.py:128
  91.4 21.9 %copy-start.5 = (f32[3,3,512]{2,1,0:T(4,128)S(1)}, f32[3,3,512]{2,1,0:T(4,128)}, u32[]{:S(2)}) copy-start(f32[3,3,512]{2,1,0:T(4,128)} %param.9) | copy-start | bytes 55300
  109.7 4.9 collective-permute-start
  149.5 2.7 copy-start.1
  164.3 18.6 %all-to-all-start = ((bf16[4,2,65536]{2,1,0:T(2,128)(2,1)}), bf16[4,2,65536]{2,1,0:T(2,128)(2,1)S(1)}, u32[]{:S(2)}, u32[]{:S(2)}) async-start(bf16[4,2,65536]{2,1,0:T(2,128)(2,1)} %reshape.261), calls=%async_computation | async-start | bytes 2097152 | tf_op jit(solution)/shard_map/all_to_all | solution.py:149
  192.8 52.6 %all-to-all-start.1 = ((bf16[2,8,512,256]{3,2,0,1:T(8,128)(2,1)}), bf16[2,8,512,256]{3,2,0,1:T(8,128)(2,1)}, u32[]{:S(2)}, u32[]{:S(2)}) async-start(bf16[2,8,512,256]{3,2,0,1:T(8,128)(2,1)} %copy.96), calls=%async_computation.1 | async-start | bytes 8388608 | tf_op jit(solution)/shard_map/all_to_all | solution.py:154
  197.6 338.3 %reduce-scatter.2.cloned.1.call-start = ((), (), s32[]{:S(2)}) async-start(), calls=%async_computation.6 | async-start | bytes 9437184 | tf_op jit(solution)/shard_map/reduce_scatter | solution.py:173
  261.6 4.0 copy-start
  261.6 4.0 copy-start.3
  283.8 5.1 copy-start.2
  438.7 2.2 copy-start.6
  449.5 86.5 %copy-start.4 = (bf16[128,4096]{1,0:T(8,128)(2,1)S(1)}, bf16[128,4096]{1,0:T(8,128)(2,1)}, u32[]{:S(2)}) copy-start(bf16[128,4096]{1,0:T(8,128)(2,1)} %param.6) | copy-start | bytes 3145732
Sparse Core Ops, SparseCore 0:
  10.7 80.5 all-gather.1
  449.7 86.2 reduce-scatter.1
where the time goes:
time: 556 us; the launch traced here: 545 us
  waiting for transfers between devices  193 us (35%)
  local copies, waits for them, and re-layouts  122 us (22%)
  matrix products  112 us (20%)
  blocking collectives  66 us (12%)
  other arithmetic  25.3 us (5%)
  between operations  14.1 us (3%)
  starting transfers between devices  13.5 us (2%)
    reduce_scatter x1, waiting for transfers between devices, per_device(): lax.psum_scatter(jnp.dot(gated, out_weight, preferred_element_type=jnp.fl...  86.4 us
    all_gather x1, waiting for transfers between devices, per_device(): lax.all_gather(normed, 'tensor', axis=0, tiled=True)  63.9 us
    all_to_all x1, blocking collectives, per_device(): lax.all_to_all(jnp.stack([real_part, imag_part]).astype(jnp.bfloat16), 's...  51.1 us
    unnamed x22, local copies, waits for them, and re-layouts  34.9 us
    all_to_all x1, waiting for transfers between devices, per_device(): lax.all_to_all(partial_spec.astype(jnp.bfloat16), 'seq', split_axis=1, co...  27.7 us
    slice x4, local copies, waits for them, and re-layouts, per_device(): extended[TAPS - 1 - offset:TAPS - 1 - offset + rows]  26.9 us
    dot_general x4, matrix products, twist(): sin_real = jnp.einsum(form, table_sin, real_part, precision=TABLE_PRECISION)  24.3 us
    dot_general x1, matrix products, per_device(): jnp.dot(lax.all_gather(normed, 'tensor', axis=0, tiled=True), flat_weight...  18.3 us
  transfers between devices with their start and end apart: 5, of which 5 were waited for; matrix products, arithmetic and copies ran while one was open for 7% of the time, Pallas kernels for 0%

commit v1 on v0

v1 whole, which is shorter than its diff:
```python
import functools

import jax
import jax.numpy as jnp
import numpy as np
from jax import lax
from jax.experimental import pallas as pl
from jax.experimental.pallas import tpu as pltpu
from jax.sharding import PartitionSpec as P

TAPS = 3
EPS = 1e-06
HALO = 16
COLUMNS = 256
VMEM_LIMIT = 56 * 1024 * 1024


def turn(count, total, index):
    angle = 2.0 * np.pi * ((np.asarray(count) * np.asarray(index)) % total) / total
    return np.cos(angle), np.sin(angle)


def short_kernel(seq_count, proj_ref, carried_ref, taps_ref, queries_ref, product_ref):
    width = queries_ref.shape[1]
    piece = width // seq_count

    def branch(j, begin):
        columns = pl.ds(j * width + begin, piece)
        ext = jnp.concatenate(
            [carried_ref[:, columns].astype(jnp.float32), proj_ref[:, columns].astype(jnp.float32)],
            axis=0,
        )
        taps = taps_ref[:, j, pl.ds(begin, piece)]
        total = ext[HALO:] * taps[0:1]
        for offset in range(1, TAPS):
            total = total + pltpu.roll(ext, offset, 0)[HALO:] * taps[offset : offset + 1]
        return total

    for place in range(seq_count):
        begin = place * piece
        queries_ref[:, pl.ds(begin, piece)] = branch(0, begin)
        product_ref[place] = (branch(1, begin) * branch(2, begin)).astype(jnp.bfloat16)


def short_products(projected, carried, short_filter, seq_count):
    rows, total_width = projected.shape
    width = total_width // 3
    return pl.pallas_call(
        functools.partial(short_kernel, seq_count),
        out_shape=(
            jax.ShapeDtypeStruct((rows, width), jnp.float32),
            jax.ShapeDtypeStruct((seq_count, rows, width // seq_count), jnp.bfloat16),
        ),
        in_specs=[pl.BlockSpec(memory_space=pltpu.VMEM)] * 3,
        out_specs=[pl.BlockSpec(memory_space=pltpu.VMEM)] * 2,
        compiler_params=pltpu.CompilerParams(vmem_limit_bytes=VMEM_LIMIT),
        cost_estimate=pl.CostEstimate(
            flops=20 * rows * width, bytes_accessed=12 * rows * width, transcendentals=0
        ),
        name="short_products",
    )(projected, carried, short_filter)


def mixed(terms):
    total = None
    for weight, value in terms:
        if abs(weight) < 1e-12:
            continue
        if abs(abs(weight) - 1.0) < 1e-12:
            term = value if weight > 0 else -value
        else:
            term = value * np.float32(weight)
        total = term if total is None else total + term
    return total


def conv_kernel(
    x_ref, g_ref, cos_ref, sin_ref, turn_cos_ref, turn_sin_ref, out_ref, xt, y_real, y_imag, z_real, z_imag
):
    count, rows, piece = x_ref.shape
    classes = count + 1
    freq_count = 2 * count
    total_length = freq_count * rows
    for s in range(count):
        xt[s] = x_ref[s].astype(jnp.float32).T
    for tile in range(rows // COLUMNS):
        columns = pl.ds(tile * COLUMNS, COLUMNS)
        blocks = [xt[s, :, columns] for s in range(count)]
        for r in range(classes):
            cos_r, sin_r = turn(r, freq_count, np.arange(count))
            real = mixed([(cos_r[s], blocks[s]) for s in range(count)])
            imag = mixed([(-sin_r[s], blocks[s]) for s in range(count)])
            turn_cos = turn_cos_ref[r : r + 1, columns]
            turn_sin = turn_sin_ref[r : r + 1, columns]
            if imag is None:
                turned_real, turned_imag = real * turn_cos, -(real * turn_sin)
            else:
                turned_real = real * turn_cos + imag * turn_sin
                turned_imag = imag * turn_cos - real * turn_sin
            y_real[pl.ds(r * piece, piece), columns] = turned_real.astype(jnp.bfloat16)
            y_imag[pl.ds(r * piece, piece), columns] = turned_imag.astype(jnp.bfloat16)

    def dot(a, b):
        return jnp.dot(a, b, preferred_element_type=jnp.float32)

    @pl.loop(0, rows // COLUMNS)
    def _(tile):
        columns = pl.ds(pl.multiple_of(tile * COLUMNS, COLUMNS), COLUMNS)
        table_cos, table_sin = cos_ref[:, columns], sin_ref[:, columns]
        for r in range(classes):
            place = pl.ds(r * piece, piece)
            real_in, imag_in = y_real[place], y_imag[place]
            if r == 0:
                real = dot(real_in, table_cos)
                imag = -dot(real_in, table_sin)
            else:
                real = dot(real_in, table_cos) + dot(imag_in, table_sin)
                imag = dot(imag_in, table_cos) - dot(real_in, table_sin)
            g_real = g_ref[0, r, :, columns].astype(jnp.float32)
            g_imag = g_ref[1, r, :, columns].astype(jnp.float32)
            z_real[place, columns] = (real * g_real - imag * g_imag).astype(jnp.bfloat16)
            z_imag[place, columns] = (real * g_imag + imag * g_real).astype(jnp.bfloat16)

    @pl.loop(0, rows // COLUMNS)
    def _(tile):
        columns = pl.ds(pl.multiple_of(tile * COLUMNS, COLUMNS), COLUMNS)
        table_cos, table_sin = cos_ref[:, columns], sin_ref[:, columns]
        sums = [None] * count
        for r in range(classes):
            place = pl.ds(r * piece, piece)
            real_in, imag_in = z_real[place], z_imag[place]
            real = dot(real_in, table_cos) - dot(imag_in, table_sin)
            if r == 0:
                turned_real, turned_imag = real, None
            else:
                imag = dot(imag_in, table_cos) + dot(real_in, table_sin)
                turn_cos = turn_cos_ref[r : r + 1, columns]
                turn_sin = turn_sin_ref[r : r + 1, columns]
                turned_real = real * turn_cos - imag * turn_sin
                turned_imag = imag * turn_cos + real * turn_sin
            cos_r, sin_r = turn(r, freq_count, np.arange(count))
            for s in range(count):
                terms = [(1.0, sums[s])] if sums[s] is not None else []
                terms += [(cos_r[s], turned_real), (-sin_r[s], turned_imag)]
                sums[s] = mixed(terms)
        for s in range(count):
            out_ref[s, columns, :] = (sums[s] * np.float32(1.0 / total_length)).T.astype(jnp.bfloat16)


def long_convolution(blocks, response, tables):
    count, rows, piece = blocks.shape
    classes = count + 1
    flops = (16 * classes) * piece * rows * rows
    return pl.pallas_call(
        conv_kernel,
        out_shape=jax.ShapeDtypeStruct((count, rows, piece), jnp.bfloat16),
        in_specs=[pl.BlockSpec(memory_space=pltpu.VMEM)] * 6,
        out_specs=pl.BlockSpec(memory_space=pltpu.VMEM),
        scratch_shapes=[
            pltpu.VMEM((count, piece, rows), jnp.float32),
            pltpu.VMEM((classes * piece, rows), jnp.bfloat16),
            pltpu.VMEM((classes * piece, rows), jnp.bfloat16),
            pltpu.VMEM((classes * piece, rows), jnp.bfloat16),
            pltpu.VMEM((classes * piece, rows), jnp.bfloat16),
        ],
        compiler_params=pltpu.CompilerParams(vmem_limit_bytes=VMEM_LIMIT),
        cost_estimate=pl.CostEstimate(
            flops=flops, bytes_accessed=4 * rows * rows + 4 * classes * piece * rows, transcendentals=0
        ),
        name="long_convolution",
    )(blocks, response, *tables)


def folded_response(filter_spectrum):
    sent = filter_spectrum.astype(jnp.bfloat16)
    spectrum = lax.all_to_all(sent, "seq", split_axis=2, concat_axis=1, tiled=True)
    freq_count, rows = spectrum.shape[1], spectrum.shape[3]
    half = freq_count // 2
    mirror = np.eye(rows, dtype=np.float32)[::-1]
    upper = jnp.einsum(
        "ckej,jm->ckem",
        spectrum[:, half + 1 :][:, ::-1],
        jnp.asarray(mirror, jnp.bfloat16),
        preferred_element_type=jnp.float32,
    )
    upper = upper * jnp.array([1.0, -1.0], jnp.float32)[:, None, None, None]
    middle = (spectrum[:, 1:half].astype(jnp.float32) + upper).astype(jnp.bfloat16)
    return jnp.concatenate([spectrum[:, :1], middle, spectrum[:, half : half + 1]], axis=1)


def dft_tables(rows, count):
    index = np.arange(rows)
    table_cos, table_sin = turn(index[:, None], rows, index[None, :])
    classes = np.arange(count + 1)
    turn_cos, turn_sin = turn(classes[:, None], 2 * count * rows, index[None, :])
    return (
        jnp.asarray(table_cos, jnp.bfloat16),
        jnp.asarray(table_sin, jnp.bfloat16),
        jnp.asarray(turn_cos, jnp.float32),
        jnp.asarray(turn_sin, jnp.float32),
    )


def per_device(tokens, norm_gain, in_weight, short_filter, filter_spectrum, out_weight):
    seq_count = lax.axis_size("seq")
    inputs = tokens.astype(jnp.float32)
    square_mean = jnp.mean(inputs * inputs, axis=-1, keepdims=True)
    normed = (inputs / jnp.sqrt(square_mean + EPS) * norm_gain).astype(jnp.bfloat16)
    model_width = in_weight.shape[0]
    width = in_weight.shape[2]
    gathered = lax.all_gather(normed, "tensor", axis=0, tiled=True)
    rows = gathered.shape[0]
    response = folded_response(filter_spectrum)
    tables = dft_tables(rows, seq_count)
    flat_weight = in_weight.reshape(model_width, 3 * width)
    gathered, response, flat_weight = lax.optimization_barrier((gathered, response, flat_weight))
    projected = jnp.dot(gathered, flat_weight, preferred_element_type=jnp.float32).astype(jnp.bfloat16)
    route = [(i, i + 1) for i in range(seq_count - 1)]
    carried = lax.ppermute(projected[rows - HALO :], "seq", route)
    queries, product = short_products(projected, carried, short_filter, seq_count)
    blocks = lax.all_to_all(product, "seq", split_axis=0, concat_axis=0, tiled=True)
    values = long_convolution(blocks, response, tables)
    returned = lax.all_to_all(values, "seq", split_axis=0, concat_axis=0, tiled=True)
    long_conv = returned.transpose(1, 0, 2).reshape(rows, width).astype(jnp.float32)
    gated = (queries * long_conv).astype(jnp.bfloat16)
    summed = lax.psum_scatter(
        jnp.dot(gated, out_weight, preferred_element_type=jnp.float32).astype(jnp.bfloat16),
        "tensor",
        scatter_dimension=0,
        tiled=True,
    ).astype(jnp.float32)
    return (inputs + summed).astype(jnp.bfloat16)


def solution(mesh):
    in_specs = (
        P(("seq", "tensor"), None),
        P(),
        P(None, None, "tensor"),
        P(None, None, "tensor"),
        P(None, "seq", "tensor", None),
        P("tensor", None),
    )
    out_specs = P(("seq", "tensor"), None)
    return jax.shard_map(
        per_device, mesh=mesh, in_specs=in_specs, out_specs=out_specs, check_vma=False
    )
```

time: 556 us -> 290 us (0.52)
  local copies, waits for them, and re-layouts: 122 us -> 37.1 us
  matrix products: 112 us -> 30.7 us
  waiting for transfers between devices: 193 us -> 127 us
  blocking collectives: 66 us -> 35.9 us
  Pallas kernels: 0 us -> 23.1 us
  other arithmetic: 25.3 us -> 8.48 us
    dot_general x21 -> x2, matrix products: 103 us -> 20.1 us  [the longest x1 18.3 us: per_device(): jnp.dot(gathered, flat_weight, preferred_element_type=jnp.float32)]
    slice x12 -> x2, local copies, waits for them, and re-layouts: 58.5 us -> 0.08 us  [the longest x1 0.07 us: folded_response(): spectrum[:, :1]]
    all_gather x1, waiting for transfers between devices: 63.9 us -> 8.75 us  [per_device(): gathered = lax.all_gather(normed, 'tensor', axis=0, tiled=True)]
    all_to_all x2, blocking collectives: 66 us -> 35.9 us  [the longest x1 19.2 us: per_device(): lax.all_to_all(product, 'seq', split_axis=0, concat_axis=0, tiled=True)]
    pallas_call x0 -> x2, Pallas kernels: none -> 23.1 us  [the longest x1 17.8 us: long_convolution(): pl.pallas_call(conv_kernel, out_shape=jax.ShapeDtypeStruct((count, rows,...]
    all_to_all x2 -> x1, waiting for transfers between devices: 41.2 us -> 30.5 us  [folded_response(): lax.all_to_all(sent, 'seq', split_axis=2, concat_axis=1, tiled=True)]
    another operation x2 -> x0, local copies, waits for them, and re-layouts: 9.17 us -> none  [the longest x1 6.26 us: per_device(): jnp.stack([real_part, imag_part]).astype(jnp.bfloat16)]
    add x3 -> x0, other arithmetic: 7.13 us -> none  [the longest x1 7.13 us: per_device(): short + short_filter[offset] * extended[TAPS - 1 - offset:TAPS - 1 - offs...]
  transfers between devices with their start and end apart: 5 -> 4, of which waited for: 5 -> 4; matrix products, arithmetic and copies ran while one was open for 7% -> 13% of each run, Pallas kernels for 0% -> 0%
where the time goes in v1:
time: 290 us; the launch traced here: 285 us
  waiting for transfers between devices  127 us (44%)
  local copies, waits for them, and re-layouts  37.1 us (13%)
  blocking collectives  35.9 us (12%)
  matrix products  30.7 us (11%)
  Pallas kernels  23.1 us (8%)
  between operations  13.5 us (5%)
  starting transfers between devices  8.62 us (3%)
  other arithmetic  8.48 us (3%)
    reduce_scatter x1, waiting for transfers between devices, per_device(): lax.psum_scatter(jnp.dot(gated, out_weight, preferred_element_type=jnp.fl...  86.4 us
    all_to_all x1, waiting for transfers between devices, folded_response(): lax.all_to_all(sent, 'seq', split_axis=2, concat_axis=1, tiled=True)  30.5 us
    unnamed x12, local copies, waits for them, and re-layouts  29.6 us
    all_to_all x1, blocking collectives, per_device(): lax.all_to_all(product, 'seq', split_axis=0, concat_axis=0, tiled=True)  19.2 us
    dot_general x1, matrix products, per_device(): jnp.dot(gathered, flat_weight, preferred_element_type=jnp.float32)  18.3 us
    pallas_call x1, Pallas kernels, long_convolution(): pl.pallas_call(conv_kernel, out_shape=jax.ShapeDtypeStruct((count, rows,...  17.8 us
    all_to_all x1, blocking collectives, per_device(): lax.all_to_all(values, 'seq', split_axis=0, concat_axis=0, tiled=True)  16.7 us
    dot_general x1, matrix products, per_device(): jnp.dot(gated, out_weight, preferred_element_type=jnp.float32)  10.6 us
  transfers between devices with their start and end apart: 4, of which 4 were waited for; matrix products, arithmetic and copies ran while one was open for 13% of the time, Pallas kernels for 0%

profile of v1, /device:TPU:8, one launch (start us, length us, event | category | flops | bytes accessed | tf_op | source)
XLA Modules:
  0.0 284.8 jit_solution(11021458765784696141)
XLA Ops:
  6.5 0.0 all-gather.2.cloned.1.call-start
  6.5 1.5 fusion.1
  8.1 2.5 fusion.3
  10.6 0.0 all-gather.2.cloned.1.call-update
  10.6 12.0 %copy.29 = bf16[2,2,512,1024]{3,1,0,2:T(2,128)(2,1)} copy(f32[2,2,512,1024]{3,2,1,0:T(8,128)} %param.16) | data formatting | bytes 12582912 | tf_op args[4]
  22.6 4.8 %all-to-all-start = ((bf16[2,2,512,1024]{3,1,0,2:T(2,128)(2,1)}), bf16[2,2,512,1024]{3,1,0,2:T(2,128)(2,1)}, u32[]{:S(2)}, u32[]{:S(2)}) async-start(bf16[2,2,512,1024]{3,1,0,2:T(2,128)(2,1)} %copy.29), calls=%async_computation | async-start | bytes 8388608 | tf_op jit(solution)/shard_map/all_to_all | solution.py:176
  27.4 0.2 reduce-scatter.2.cloned.1.call-start
  27.7 17.0 %copy.23 = bf16[4096,3,512]{0,2,1:T(8,128)(2,1)} copy(bf16[4096,3,512]{2,0,1:T(8,128)(2,1)} %param.14) | data formatting | bytes 25165824 | tf_op args[2]
  44.7 30.5 %all-to-all-done = bf16[2,2,512,1024]{3,1,0,2:T(2,128)(2,1)} async-done(((bf16[2,2,512,1024]{3,1,0,2:T(2,128)(2,1)}), bf16[2,2,512,1024]{3,1,0,2:T(2,128)(2,1)}, u32[]{:S(2)}, u32[]{:S(2)}) %all-to-all-start) | async-done | bytes 4194336 | tf_op jit(solution)/shard_map/all_to_all | solution.py:176
  75.1 0.0 copy-start.3
  75.1 0.0 copy-start.4
  75.1 3.7 %copy.21 = bf16[2,2,4,128,1024]{4,3,1,2,0:T(8,128)(2,1)S(1)} copy(bf16[2,2,4,128,1024]{4,1,0,3,2:T(2,128)(2,1)} %bitcast) | data formatting | bytes 8388608 | tf_op jit(solution)/shard_map/all_to_all | solution.py:176
  78.8 0.1 fusion.6
  78.9 0.0 copy-done.3
  78.9 0.0 copy-done.4
  78.9 1.8 fusion
  80.8 1.8 pad_maximum_fusion.g_ref
  82.6 8.7 %all-gather.2.cloned.1.call-done = bf16[1024,4096]{1,0:T(8,128)(2,1)} async-done(((bf16[128,4096]{1,0:T(8,128)(2,1)}), bf16[1024,4096]{1,0:T(8,128)(2,1)}) %all-gather.2.cloned.1.call-update) | async-done | bytes 8388624 | tf_op jit(solution)/shard_map/all_gather | solution.py:211
  91.4 18.3 %convolution_convert_fusion.1.proj_ref = bf16[1024,1536]{1,0:T(8,128)(2,1)S(1)} fusion(bf16[1024,4096]{1,0:T(8,128)(2,1)} %all-gather.2.cloned.1.call-done, bf16[4096,1536]{0,1:T(8,128)(2,1)} %bitcast.19), kind=kOutput, calls=%fused_computation.2 | convolution fusion | flops 12886474752 | bytes 24117248 | tf_op jit(solution)/shard_map/dot_general | solution.py:217
  109.6 0.0 copy-start.1
  109.6 3.6 %collective-permute-start = (bf16[16,1536]{1,0:T(8,128)(2,1)S(1)}, bf16[16,1536]{1,0:T(8,128)(2,1)S(1)}, u32[]{:S(2)}, u32[]{:S(2)}) collective-permute-start(bf16[16,1536]{1,0:T(8,128)(2,1)S(1)} %slice.24), channel_id=1, source_target_pairs={{0,8},{8,16},{16,24},{1,9},{9,17},{17,25},{2,10},{10,18},{18,26},{... | collective-permute-start | bytes 147464 | tf_op jit(solution)/shard_map/ppermute | solution.py:219
  113.2 1.7 collective-permute-done.carried_ref
  115.0 0.0 copy-done.1
  115.0 0.0 copy-start.2
  115.0 0.6 copy-done.2
  115.6 5.3 %short_products.1 = (f32[1024,512]{1,0:T(8,128)}, bf16[4,1024,128]{2,1,0:T(8,128)(2,1)}) custom-call(bf16[1024,1536]{1,0:T(8,128)(2,1)} %copy-done.1, bf16[16,1536]{1,0:T(8,128)(2,1)} %copy-done.2, f32[3,3,512]{2,1,0:T(4,128)} %taps_ref.1), custom_call_target="tpu_custom_call" | custom-call | flops 10485760 | bytes 6291456 | tf_op jit(solution)/shard_map/short_products/pallas_call | solution.py:48
  120.9 19.2 %all_to_all.28.x_ref = bf16[4,1024,128]{2,1,0:T(8,128)(2,1)} all-to-all(bf16[4,1024,128]{2,1,0:T(8,128)(2,1)} %get-tuple-element.13), channel_id=1, replica_groups=mesh['seq'=4,'tensor'=8] {'seq'}, dimensions={0} | all-to-all | bytes 2097152 | tf_op jit(solution)/shard_map/all_to_all | solution.py:221
  140.1 17.8 %long_convolution.1 = bf16[4,1024,128]{2,1,0:T(8,128)(2,1)} custom-call(bf16[4,1024,128]{2,1,0:T(8,128)(2,1)} %all_to_all.28.x_ref, bf16[2,5,128,1024]{3,2,1,0:T(8,128)(2,1)} %pad_maximum_fusion.g_ref, bf16[1024,1024]{1,0:T(8,128)(2,1)} %constant.21.clone.cos_ref, bf16[1024,1024]{1,0:T(8,128)(2,1)} %constant.22.clone.sin_ref, ...), custom_call_target="tpu_custom_call" | custom-call | flops 10737418240 | bytes 6815744 | tf_op jit(solution)/shard_map/long_convolution/pallas_call | solution.py:154
  157.9 16.7 %all_to_all.29 = bf16[4,1024,128]{2,1,0:T(8,128)(2,1)S(1)} all-to-all(bf16[4,1024,128]{2,1,0:T(8,128)(2,1)} %long_convolution.1), channel_id=1, replica_groups=mesh['seq'=4,'tensor'=8] {'seq'}, dimensions={0} | all-to-all | bytes 2097152 | tf_op jit(solution)/shard_map/all_to_all | solution.py:223
  174.6 0.1 convert_bitcast_fusion
  174.7 1.9 copy.24
  176.6 1.9 copy.25
  178.5 10.6 %convolution_convert_fusion = bf16[1024,4096]{1,0:T(8,128)(2,1)} fusion(bf16[512,4096]{1,0:T(8,128)(2,1)} %param.17, f32[1024,512]{1,0:T(8,128)} %get-tuple-element.12, f32[1024,512]{1,0:T(8,128)S(1)} %copy.25), kind=kOutput, calls=%fused_computation.1 | convolution fusion | flops 4300210176 | bytes 16777216 | tf_op jit(solution)/shard_map/dot_general | solution.py:227
  189.1 0.0 copy-start
  189.1 0.0 reduce-scatter.2.cloned.1.call-update
  189.1 86.4 %reduce-scatter.2.cloned.1.call-done = bf16[128,4096]{1,0:T(8,128)(2,1)} async-done(((bf16[1024,4096]{1,0:T(8,128)(2,1)}), bf16[128,4096]{1,0:T(8,128)(2,1)}) %reduce-scatter.2.cloned.1.call-update) | async-done | bytes 1048592 | tf_op jit(solution)/shard_map/reduce_scatter | solution.py:226
  275.5 0.0 copy-done
  275.5 2.4 fusion.4
  (2 shorter events, 0.0 us)
Async XLA Ops:
  6.5 84.8 %all-gather.2.cloned.1.call-start = ((), (), s32[]{:S(2)}) async-start(), calls=%async_computation.4 | async-start | bytes 9437184 | tf_op jit(solution)/shard_map/all_gather | solution.py:211
  22.6 52.5 %all-to-all-start = ((bf16[2,2,512,1024]{3,1,0,2:T(2,128)(2,1)}), bf16[2,2,512,1024]{3,1,0,2:T(2,128)(2,1)}, u32[]{:S(2)}, u32[]{:S(2)}) async-start(bf16[2,2,512,1024]{3,1,0,2:T(2,128)(2,1)} %copy.29), calls=%async_computation | async-start | bytes 8388608 | tf_op jit(solution)/shard_map/all_to_all | solution.py:176
  27.4 248.1 %reduce-scatter.2.cloned.1.call-start = ((), (), s32[]{:S(2)}) async-start(), calls=%async_computation.5 | async-start | bytes 9437184 | tf_op jit(solution)/shard_map/reduce_scatter | solution.py:226
  75.1 3.8 %copy-start.3 = (bf16[1024,1024,1,1]{0,1,3,2:T(8,128)(2,1)S(1)}, bf16[1024,1024,1,1]{0,1,3,2:T(8,128)(2,1)}, u32[]{:S(2)}) copy-start(bf16[1024,1024,1,1]{0,1,3,2:T(8,128)(2,1)} %constant.26) | copy-start | bytes 6291460
  75.1 3.8 %copy-start.4 = (f32[2]{0:T(128)S(1)}, f32[2]{0:T(128)}, u32[]{:S(2)}) copy-start(f32[2]{0:T(128)} %constant.20.clone) | copy-start | bytes 28
  109.6 5.3 %copy-start.1 = (bf16[1024,1536]{1,0:T(8,128)(2,1)}, bf16[1024,1536]{1,0:T(8,128)(2,1)S(1)}, u32[]{:S(2)}) copy-start(bf16[1024,1536]{1,0:T(8,128)(2,1)S(1)} %convolution_convert_fusion.1.proj_ref) | copy-start | bytes 9437188
  109.6 5.3 %collective-permute-start = (bf16[16,1536]{1,0:T(8,128)(2,1)S(1)}, bf16[16,1536]{1,0:T(8,128)(2,1)S(1)}, u32[]{:S(2)}, u32[]{:S(2)}) collective-permute-start(bf16[16,1536]{1,0:T(8,128)(2,1)S(1)} %slice.24), channel_id=1, source_target_pairs={{0,8},{8,16},{16,24},{1,9},{9,17},{17,25},{2,10},{10,18},{18,26},{... | collective-permute-start | bytes 147464 | tf_op jit(solution)/shard_map/ppermute | solution.py:219
  115.0 0.6 copy-start.2
  189.1 86.5 %copy-start = (bf16[128,4096]{1,0:T(8,128)(2,1)S(1)}, bf16[128,4096]{1,0:T(8,128)(2,1)}, u32[]{:S(2)}) copy-start(bf16[128,4096]{1,0:T(8,128)(2,1)} %param.12) | copy-start | bytes 3145732
Sparse Core Ops, SparseCore 0:
  10.7 80.5 all-gather.1
  189.2 86.2 reduce-scatter.1

commit v2 on v1

--- a/solution.py
+++ b/solution.py
@@ -20,14 +20,213 @@
     return np.cos(angle), np.sin(angle)
 
 
+MESH = pl.DeviceIdType.MESH
+CHUNKS = 4
+
+
+def gather_kernel(
+    seq_count, tensor_count, normed_ref, weight_ref, filter_ref, proj_ref, spectrum_ref,
+    held, weights, weight_sem, own_sem, filter_send, filter_recv, recv, to_right, to_left, to_sibling,
+):
+    seq_place = lax.axis_index("seq")
+    place = lax.axis_index("tensor")
+    chips = tensor_count // 2
+    chip, core = place // 2, place % 2
+    sibling = chip * 2 + 1 - core
+    has_right, has_left = chip < chips - 1, chip > 0
+    right, left = place + 2, place - 2
+    size = held.shape[1]
+    step = size // CHUNKS
+    classes = filter_ref.shape[1]
+    piece = spectrum_ref.shape[2]
+    width = weight_ref.shape[2]
+
+    weight_copy = pltpu.make_async_copy(weight_ref, weights, weight_sem)
+    weight_copy.start()
+    own_filter = pltpu.make_async_copy(
+        filter_ref.at[:, :, pl.ds(seq_place * piece, piece), :],
+        spectrum_ref.at[:, pl.ds(seq_place * classes, classes), :, :],
+        own_sem,
+    )
+    own_filter.start()
+    held[place] = normed_ref[...]
+
+    barrier = pltpu.get_barrier_semaphore()
+    pl.semaphore_signal(barrier, inc=1, device_id={"tensor": sibling}, device_id_type=MESH)
+
+    @pl.when(has_right)
+    def _():
+        pl.semaphore_signal(barrier, inc=1, device_id={"tensor": right}, device_id_type=MESH)
+
+    @pl.when(has_left)
+    def _():
+        pl.semaphore_signal(barrier, inc=1, device_id={"tensor": left}, device_id_type=MESH)
+
+    for k in range(1, seq_count):
+        peer = lax.rem(seq_place + k, seq_count)
+        pl.semaphore_signal(barrier, inc=1, device_id={"seq": peer}, device_id_type=MESH)
+    neighbours = has_right.astype(jnp.int32) + has_left.astype(jnp.int32)
+    pl.semaphore_wait(barrier, seq_count + neighbours)
+
+    def passed(block, q, target, send_sem):
+        part = held.at[block, pl.ds(q * step, step)]
+        return pltpu.make_async_remote_copy(
+            src_ref=part,
+            dst_ref=part,
+            send_sem=send_sem.at[block, q],
+            recv_sem=recv.at[block, q],
+            device_id={"tensor": target},
+            device_id_type=MESH,
+        )
+
+    def filter_copy(k):
+        peer = lax.rem(seq_place + k, seq_count)
+        return pltpu.make_async_remote_copy(
+            src_ref=filter_ref.at[:, :, pl.ds(peer * piece, piece), :],
+            dst_ref=spectrum_ref.at[:, pl.ds(seq_place * classes, classes), :, :],
+            send_sem=filter_send.at[k],
+            recv_sem=filter_recv.at[k],
+            device_id={"seq": peer},
+            device_id_type=MESH,
+        )
+
+    def multiply(other):
+        for q in range(CHUNKS):
+            passed(other * 2 + 1 - core, q, sibling, to_sibling).wait_recv()
+        rows = pl.ds(pl.multiple_of(other * 2 * size, 2 * size), 2 * size)
+
+        @pl.loop(0, 3)
+        def _(j):
+            for begin in range(0, width, 256):
+                columns = min(256, width - begin)
+                value = jnp.dot(
+                    held[pl.ds(other * 2, 2)].reshape(2 * size, held.shape[2]),
+                    weights[j, :, pl.ds(begin, columns)],
+                    preferred_element_type=jnp.float32,
+                )
+                proj_ref[j, rows, pl.ds(begin, columns)] = value.astype(jnp.bfloat16)
+
+    for q in range(CHUNKS):
+
+        @pl.when(has_right)
+        def _():
+            passed(place, q, right, to_right).start()
+
+        @pl.when(has_left)
+        def _():
+            passed(place, q, left, to_left).start()
+
+        passed(place, q, sibling, to_sibling).start()
+    for k in range(1, seq_count):
+        filter_copy(k).start()
+    weight_copy.wait()
+    multiply(chip)
+
+    def sides(distance):
+        yield chip + distance, chip + distance < chips, right, has_left, left, to_left
+        yield chip - distance, chip - distance >= 0, left, has_right, right, to_right
+
+    @pl.loop(1, chips)
+    def _(distance):
+        for q in range(CHUNKS):
+            for other, exists, source, onward, target, send_sem in sides(distance):
+
+                @pl.when(exists)
+                def _():
+                    block = other * 2 + core
+                    passed(block, q, source, send_sem).wait_recv()
+
+                    @pl.when(onward)
+                    def _():
+                        passed(block, q, target, send_sem).start()
+
+                    passed(block, q, sibling, to_sibling).start()
+
+        for other, exists, *_rest in sides(distance):
+
+            @pl.when(exists)
+            def _():
+                multiply(other)
+
+    for q in range(CHUNKS):
+
+        @pl.when(has_right)
+        def _():
+            passed(place, q, right, to_right).wait_send()
+
+        @pl.when(has_left)
+        def _():
+            passed(place, q, left, to_left).wait_send()
+
+        passed(place, q, sibling, to_sibling).wait_send()
+
+    @pl.loop(1, chips)
+    def _(distance):
+        for q in range(CHUNKS):
+            for other, exists, source, onward, target, send_sem in sides(distance):
+
+                @pl.when(exists)
+                def _():
+                    block = other * 2 + core
+
+                    @pl.when(onward)
+                    def _():
+                        passed(block, q, target, send_sem).wait_send()
+
+                    passed(block, q, sibling, to_sibling).wait_send()
+
+    for k in range(1, seq_count):
+        filter_copy(k).wait()
+    own_filter.wait()
+
+
+def gathered_projection(normed, weight, filters, seq_count, tensor_count):
+    size, model_width = normed.shape
+    width = weight.shape[2]
+    parts, classes, channels, freqs = filters.shape
+    rows = size * tensor_count
+    blocks = pltpu.SemaphoreType.DMA((tensor_count, CHUNKS))
+    return pl.pallas_call(
+        functools.partial(gather_kernel, seq_count, tensor_count),
+        out_shape=(
+            jax.ShapeDtypeStruct((3, rows, width), jnp.bfloat16),
+            jax.ShapeDtypeStruct(
+                (parts, classes * seq_count, channels // seq_count, freqs), jnp.bfloat16
+            ),
+        ),
+        in_specs=[
+            pl.BlockSpec(memory_space=pltpu.VMEM),
+            pl.BlockSpec(memory_space=pl.ANY),
+            pl.BlockSpec(memory_space=pl.ANY),
+        ],
+        out_specs=[pl.BlockSpec(memory_space=pltpu.VMEM), pl.BlockSpec(memory_space=pl.ANY)],
+        scratch_shapes=[
+            pltpu.VMEM((tensor_count, size, model_width), jnp.bfloat16),
+            pltpu.VMEM(weight.shape, jnp.bfloat16),
+            pltpu.SemaphoreType.DMA,
+            pltpu.SemaphoreType.DMA,
+            pltpu.SemaphoreType.DMA((seq_count,)),
+            pltpu.SemaphoreType.DMA((seq_count,)),
+            blocks, blocks, blocks, blocks,
+        ],
+        compiler_params=pltpu.CompilerParams(
+            vmem_limit_bytes=VMEM_LIMIT, collective_id=0, has_side_effects=True
+        ),
+        cost_estimate=pl.CostEstimate(
+            flops=6 * rows * model_width * width, bytes_accessed=6 * model_width * width, transcendentals=0
+        ),
+        name="gathered_projection",
+    )(normed, weight, filters)
+
+
 def short_kernel(seq_count, proj_ref, carried_ref, taps_ref, queries_ref, product_ref):
     width = queries_ref.shape[1]
     piece = width // seq_count
 
     def branch(j, begin):
-        columns = pl.ds(j * width + begin, piece)
+        columns = pl.ds(begin, piece)
         ext = jnp.concatenate(
-            [carried_ref[:, columns].astype(jnp.float32), proj_ref[:, columns].astype(jnp.float32)],
+            [carried_ref[j, :, columns].astype(jnp.float32), proj_ref[j, :, columns].astype(jnp.float32)],
             axis=0,
         )
         taps = taps_ref[:, j, pl.ds(begin, piece)]
@@ -43,8 +242,7 @@
 
 
 def short_products(projected, carried, short_filter, seq_count):
-    rows, total_width = projected.shape
-    width = total_width // 3
+    rows, width = projected.shape[1:]
     return pl.pallas_call(
         functools.partial(short_kernel, seq_count),
         out_shape=(
@@ -171,9 +369,7 @@
     )(blocks, response, *tables)
 
 
-def folded_response(filter_spectrum):
-    sent = filter_spectrum.astype(jnp.bfloat16)
-    spectrum = lax.all_to_all(sent, "seq", split_axis=2, concat_axis=1, tiled=True)
+def folded_response(spectrum):
     freq_count, rows = spectrum.shape[1], spectrum.shape[3]
     half = freq_count // 2
     mirror = np.eye(rows, dtype=np.float32)[::-1]
@@ -206,17 +402,19 @@
     inputs = tokens.astype(jnp.float32)
     square_mean = jnp.mean(inputs * inputs, axis=-1, keepdims=True)
     normed = (inputs / jnp.sqrt(square_mean + EPS) * norm_gain).astype(jnp.bfloat16)
-    model_width = in_weight.shape[0]
     width = in_weight.shape[2]
-    gathered = lax.all_gather(normed, "tensor", axis=0, tiled=True)
-    rows = gathered.shape[0]
-    response = folded_response(filter_spectrum)
+    projected, spectrum = gathered_projection(
+        normed,
+        in_weight.transpose(1, 0, 2),
+        filter_spectrum.astype(jnp.bfloat16),
+        seq_count,
+        lax.axis_size("tensor"),
+    )
+    rows = projected.shape[1]
     tables = dft_tables(rows, seq_count)
-    flat_weight = in_weight.reshape(model_width, 3 * width)
-    gathered, response, flat_weight = lax.optimization_barrier((gathered, response, flat_weight))
-    projected = jnp.dot(gathered, flat_weight, preferred_element_type=jnp.float32).astype(jnp.bfloat16)
     route = [(i, i + 1) for i in range(seq_count - 1)]
-    carried = lax.ppermute(projected[rows - HALO :], "seq", route)
+    carried = lax.ppermute(projected[:, rows - HALO :], "seq", route)
+    response = folded_response(spectrum)
     queries, product = short_products(projected, carried, short_filter, seq_count)
     blocks = lax.all_to_all(product, "seq", split_axis=0, concat_axis=0, tiled=True)
     values = long_convolution(blocks, response, tables)

time: 290 us -> 277 us (0.955)
  Pallas kernels: 23.1 us -> 97.2 us
  waiting for transfers between devices: 127 us -> 97.6 us
  local copies, waits for them, and re-layouts: 37.1 us -> 10.2 us
  blocking collectives: 35.9 us -> 18.1 us
  matrix products: 30.7 us -> 14.9 us
  other arithmetic: 8.48 us -> 13.4 us
    pallas_call x0 -> x1, Pallas kernels: none -> 74.1 us  [gathered_projection(): pl.pallas_call(functools.partial(gather_kernel, seq_count, tensor_count),...]
    unnamed x12 -> x10, local copies, waits for them, and re-layouts: 29.6 us -> 0.64 us
    all_to_all x1, waiting for transfers between devices: 30.5 us -> 2 us  [per_device(): lax.all_to_all(product, 'seq', split_axis=0, concat_axis=0, tiled=True)]
    all_to_all x1 -> x0, blocking collectives: 19.2 us -> none  [per_device(): lax.all_to_all(product, 'seq', split_axis=0, concat_axis=0, tiled=True)]
    dot_general x1 -> x0, matrix products: 18.3 us -> none  [per_device(): jnp.dot(gathered, flat_weight, preferred_element_type=jnp.float32)]
    all_gather x1 -> x0, waiting for transfers between devices: 8.75 us -> none  [per_device(): gathered = lax.all_gather(normed, 'tensor', axis=0, tiled=True)]
    reduce_scatter x1, waiting for transfers between devices: 86.4 us -> 93.8 us  [per_device(): lax.psum_scatter(jnp.dot(gated, out_weight, preferred_element_type=jnp.fl...]
    convert_element_type x0 -> x1, other arithmetic: none -> 6.12 us  [per_device(): filter_spectrum.astype(jnp.bfloat16)]
  transfers between devices with their start and end apart: 4 -> 3, of which waited for: 4 -> 3; matrix products, arithmetic and copies ran while one was open for 13% -> 4% of each run, Pallas kernels for 0% -> 0%
where the time goes in v2:
time: 277 us; the launch traced here: 272 us
  waiting for transfers between devices  97.6 us (35%)
  Pallas kernels  97.2 us (35%)
  blocking collectives  18.1 us (7%)
  matrix products  14.9 us (5%)
  between operations  13.5 us (5%)
  other arithmetic  13.4 us (5%)
  local copies, waits for them, and re-layouts  10.2 us (4%)
  starting transfers between devices  7.07 us (3%)
    reduce_scatter x1, waiting for transfers between devices, per_device(): lax.psum_scatter(jnp.dot(gated, out_weight, preferred_element_type=jnp.fl...  93.8 us
    pallas_call x1, Pallas kernels, gathered_projection(): pl.pallas_call(functools.partial(gather_kernel, seq_count, tensor_count),...  74.1 us
    all_to_all x1, blocking collectives, per_device(): lax.all_to_all(values, 'seq', split_axis=0, concat_axis=0, tiled=True)  18.1 us
    pallas_call x1, Pallas kernels, long_convolution(): pl.pallas_call(conv_kernel, out_shape=jax.ShapeDtypeStruct((count, rows,...  17.8 us
    dot_general x1, matrix products, per_device(): jnp.dot(gated, out_weight, preferred_element_type=jnp.float32)  10.6 us
    convert_element_type x1, other arithmetic, per_device(): filter_spectrum.astype(jnp.bfloat16)  6.12 us
  transfers between devices with their start and end apart: 3, of which 3 were waited for; matrix products, arithmetic and copies ran while one was open for 4% of the time, Pallas kernels for 0%

profile of v2, /device:TPU:8, one launch (start us, length us, event | category | flops | bytes accessed | tf_op | source)
XLA Modules:
  0.0 271.9 jit_solution(17566898177727031224)
XLA Ops:
  6.5 1.5 fusion
  8.1 0.0 copy-start
  8.1 0.0 copy-start.3
  8.1 6.1 %convert_element_type.38.filter_ref = bf16[2,2,512,1024]{3,2,1,0:T(8,128)(2,1)} convert(f32[2,2,512,1024]{3,2,1,0:T(8,128)} %param.16) | non-fusion elementwise | flops 2097152 | bytes 12582912 | tf_op jit(solution)/shard_map/convert_element_type | solution.py:409
  14.2 0.0 copy-done
  14.2 0.0 copy-done.3
  14.2 1.3 fusion.2.normed_ref
  15.5 74.1 %gathered_projection.1 = (bf16[3,1024,512]{2,1,0:T(8,128)(2,1)}, bf16[2,8,128,1024]{3,2,1,0:T(8,128)(2,1)}) custom-call(bf16[128,4096]{1,0:T(8,128)(2,1)} %fusion.2.normed_ref, bf16[3,4096,512]{2,1,0:T(8,128)(2,1)} %bitcast.11, bf16[2,2,512,1024]{3,2,1,0:T(8,128)(2,1)} %convert_element_type.38.filter_ref), custom_call_target="tpu_custom_call" | custom-call | flops 12884901888 | bytes 12582912 | tf_op jit(solution)/shard_map/gathered_projection/pallas_call | solution.py:189
  89.6 0.8 slice.15
  90.4 2.5 collective-permute-start
  92.9 1.7 collective-permute-done.carried_ref
  94.7 0.0 copy-start.2
  94.7 0.6 copy-done.2
  95.3 5.3 %short_products.1 = (f32[1024,512]{1,0:T(8,128)}, bf16[4,1024,128]{2,1,0:T(8,128)(2,1)}) custom-call(bf16[3,1024,512]{2,1,0:T(8,128)(2,1)} %get-tuple-element.9.proj_ref, bf16[3,16,512]{2,1,0:T(8,128)(2,1)} %copy-done.2, f32[3,3,512]{2,1,0:T(4,128)} %taps_ref.1), custom_call_target="tpu_custom_call" | custom-call | flops 10485760 | bytes 6291456 | tf_op jit(solution)/shard_map/short_products/pallas_call | solution.py:246
  100.6 4.6 %all-to-all-start = ((bf16[4,1024,128]{2,1,0:T(8,128)(2,1)}), bf16[4,1024,128]{2,1,0:T(8,128)(2,1)}, u32[]{:S(2)}, u32[]{:S(2)}) async-start(bf16[4,1024,128]{2,1,0:T(8,128)(2,1)} %get-tuple-element.11), calls=%async_computation | async-start | bytes 2097152 | tf_op jit(solution)/shard_map/all_to_all | solution.py:419
  105.2 0.0 reduce-scatter.2.cloned.1.call-start
  105.2 2.1 fusion.4
  107.3 1.5 slice.18
  108.8 0.0 copy-start.4
  108.9 1.3 rev.3
  110.1 0.0 copy-done.4
  110.1 0.0 copy-start.1
  110.1 4.4 %add_convert_fusion = bf16[2,3,128,1024]{3,2,1,0:T(8,128)(2,1)S(1)} fusion(bf16[2,3,128,1024]{3,2,1,0:T(8,128)(2,1)} %rev.3, bf16[1024,1024,1,1]{1,0,3,2:T(8,128)(2,1)} %constant.26, f32[2]{0:T(128)S(1)} %copy-done.4, bf16[2,8,128,1024]{3,2,1,0:T(8,128)(2,1)} %get-tuple-element.12), kind=kOutput, calls=%fused_computation.1 | convolution fusion | flops 1613758464 | bytes 6815752 | tf_op jit(solution)/shard_map/ckej,jm->ckem/dot_general | solution.py:376
  114.5 0.0 copy-done.1
  114.5 1.8 pad_maximum_fusion.g_ref
  116.3 2.0 all-to-all-done.x_ref
  118.3 17.8 %long_convolution.1 = bf16[4,1024,128]{2,1,0:T(8,128)(2,1)} custom-call(bf16[4,1024,128]{2,1,0:T(8,128)(2,1)} %all-to-all-done.x_ref, bf16[2,5,128,1024]{3,2,1,0:T(8,128)(2,1)} %pad_maximum_fusion.g_ref, bf16[1024,1024]{1,0:T(8,128)(2,1)} %constant.19.clone.cos_ref, bf16[1024,1024]{1,0:T(8,128)(2,1)} %constant.20.clone.sin_ref, ...), custom_call_target="tpu_custom_call" | custom-call | flops 10737418240 | bytes 6815744 | tf_op jit(solution)/shard_map/long_convolution/pallas_call | solution.py:352
  136.1 18.1 %all_to_all.10 = bf16[4,1024,128]{2,1,0:T(8,128)(2,1)S(1)} all-to-all(bf16[4,1024,128]{2,1,0:T(8,128)(2,1)} %long_convolution.1), channel_id=1, replica_groups=mesh['seq'=4,'tensor'=8] {'seq'}, dimensions={0} | all-to-all | bytes 2097152 | tf_op jit(solution)/shard_map/all_to_all | solution.py:421
  154.2 0.1 convert_bitcast_fusion
  154.4 1.9 copy.13
  156.2 1.9 copy.14
  158.2 10.6 %convolution_convert_fusion = bf16[1024,4096]{1,0:T(8,128)(2,1)} fusion(bf16[512,4096]{1,0:T(8,128)(2,1)} %param.17, f32[1024,512]{1,0:T(8,128)} %get-tuple-element.10, f32[1024,512]{1,0:T(8,128)S(1)} %copy.14), kind=kOutput, calls=%fused_computation | convolution fusion | flops 4300210176 | bytes 16777216 | tf_op jit(solution)/shard_map/dot_general | solution.py:425
  168.7 0.0 reduce-scatter.2.cloned.1.call-update
  168.8 93.8 %reduce-scatter.2.cloned.1.call-done = bf16[128,4096]{1,0:T(8,128)(2,1)} async-done(((bf16[1024,4096]{1,0:T(8,128)(2,1)}), bf16[128,4096]{1,0:T(8,128)(2,1)}) %reduce-scatter.2.cloned.1.call-update) | async-done | bytes 1048592 | tf_op jit(solution)/shard_map/reduce_scatter | solution.py:424
  262.6 2.4 fusion.3
  (1 shorter events, 0.0 us)
Async XLA Ops:
  8.1 6.1 %copy-start = (bf16[128,4096]{1,0:T(8,128)(2,1)S(1)}, bf16[128,4096]{1,0:T(8,128)(2,1)}, u32[]{:S(2)}) copy-start(bf16[128,4096]{1,0:T(8,128)(2,1)} %param.12) | copy-start | bytes 3145732
  8.1 6.1 %copy-start.3 = (f32[4096]{0:T(1024)S(1)}, f32[4096]{0:T(1024)}, u32[]{:S(2)}) copy-start(f32[4096]{0:T(1024)} %param.13) | copy-start | bytes 49156
  90.4 4.2 %collective-permute-start = (bf16[3,16,512]{2,1,0:T(8,128)(2,1)S(1)}, bf16[3,16,512]{2,1,0:T(8,128)(2,1)S(1)}, u32[]{:S(2)}, u32[]{:S(2)}) collective-permute-start(bf16[3,16,512]{2,1,0:T(8,128)(2,1)S(1)} %slice.15), channel_id=1, source_target_pairs={{0,8},{8,16},{16,24},{1,9},{9,17},{17,25},{2,10},{10,18},{18,26},{... | collective-permute-start | bytes 147464 | tf_op jit(solution)/shard_map/ppermute | solution.py:416
  94.7 0.6 copy-start.2
  100.6 17.7 %all-to-all-start = ((bf16[4,1024,128]{2,1,0:T(8,128)(2,1)}), bf16[4,1024,128]{2,1,0:T(8,128)(2,1)}, u32[]{:S(2)}, u32[]{:S(2)}) async-start(bf16[4,1024,128]{2,1,0:T(8,128)(2,1)} %get-tuple-element.11), calls=%async_computation | async-start | bytes 2097152 | tf_op jit(solution)/shard_map/all_to_all | solution.py:419
  105.2 157.4 %reduce-scatter.2.cloned.1.call-start = ((), (), s32[]{:S(2)}) async-start(), calls=%async_computation.3 | async-start | bytes 9437184 | tf_op jit(solution)/shard_map/reduce_scatter | solution.py:424
  108.8 1.3 copy-start.4
  110.1 4.4 %copy-start.1 = (bf16[2,1,128,1024]{3,2,1,0:T(8,128)(2,1)S(1)}, bf16[2,1,128,1024]{3,2,1,0:T(8,128)(2,1)}, u32[]{:S(2)}) copy-start(bf16[2,1,128,1024]{3,2,1,0:T(8,128)(2,1)} %get-tuple-element.14) | copy-start | bytes 1572868
Sparse Core Ops, SparseCore 0:
  168.9 93.6 reduce-scatter.1

commit v3 on v2

--- a/solution.py
+++ b/solution.py
@@ -217,6 +217,174 @@
         ),
         name="gathered_projection",
     )(normed, weight, filters)
+
+
+def scatter_kernel(
+    tensor_count, tokens_ref, queries_ref, values_ref, own_ref, other_ref, out_ref,
+    gated, shared, outgoing, from_left, from_right, totals,
+    share_send, share_recv, send_right, send_left, recv_left, recv_right,
+):
+    place = lax.axis_index("tensor")
+    chips = tensor_count // 2
+    chip, core = place // 2, place % 2
+    sibling = chip * 2 + 1 - core
+    has_right, has_left = chip < chips - 1, chip > 0
+    right, left = place + 2, place - 2
+    size, model_width = tokens_ref.shape
+    step = model_width // CHUNKS
+    count, rows, piece = values_ref.shape
+
+    barrier = pltpu.get_barrier_semaphore()
+    pl.semaphore_signal(barrier, inc=1, device_id={"tensor": sibling}, device_id_type=MESH)
+
+    @pl.when(has_right)
+    def _():
+        pl.semaphore_signal(barrier, inc=1, device_id={"tensor": right}, device_id_type=MESH)
+
+    @pl.when(has_left)
+    def _():
+        pl.semaphore_signal(barrier, inc=1, device_id={"tensor": left}, device_id_type=MESH)
+
+    for s in range(count):
+        columns = pl.ds(s * piece, piece)
+        value = queries_ref[:, columns] * values_ref[s].astype(jnp.float32)
+        gated[:, :, :, columns] = value.astype(jnp.bfloat16).reshape(chips, 2, size, piece)
+
+    neighbours = has_right.astype(jnp.int32) + has_left.astype(jnp.int32)
+    pl.semaphore_wait(barrier, 1 + neighbours)
+    share = pltpu.make_async_remote_copy(
+        src_ref=gated.at[:, 1 - core],
+        dst_ref=shared,
+        send_sem=share_send,
+        recv_sem=share_recv,
+        device_id={"tensor": sibling},
+        device_id_type=MESH,
+    )
+    share.start()
+    share.wait()
+
+    def rightward(dest, q):
+        columns = pl.ds(q * step, step)
+        return pltpu.make_async_remote_copy(
+            src_ref=outgoing.at[dest, :, columns],
+            dst_ref=from_left.at[dest, :, columns],
+            send_sem=send_right.at[dest, q],
+            recv_sem=recv_left.at[dest, q],
+            device_id={"tensor": right},
+            device_id_type=MESH,
+        )
+
+    def leftward(dest, q):
+        columns = pl.ds(q * step, step)
+        return pltpu.make_async_remote_copy(
+            src_ref=outgoing.at[dest, :, columns],
+            dst_ref=from_right.at[dest, :, columns],
+            send_sem=send_left.at[dest, q],
+            recv_sem=recv_right.at[dest, q],
+            device_id={"tensor": left},
+            device_id_type=MESH,
+        )
+
+    def partial(dest, columns):
+        return jnp.dot(
+            gated[dest, core], own_ref[:, columns], preferred_element_type=jnp.float32
+        ) + jnp.dot(shared[dest], other_ref[:, columns], preferred_element_type=jnp.float32)
+
+    def tiles(q):
+        width = min(512, step)
+        for begin in range(0, step, width):
+            yield pl.ds(q * step + begin, width)
+
+    def relay(dest, q, has_more, arriving, buffer):
+        for columns in tiles(q):
+            outgoing[dest, :, columns] = partial(dest, columns).astype(jnp.bfloat16)
+
+        @pl.when(has_more)
+        def _():
+            arriving(dest, q).wait_recv()
+            for columns in tiles(q):
+                total = outgoing[dest, :, columns].astype(jnp.float32) + buffer[
+                    dest, :, columns
+                ].astype(jnp.float32)
+                outgoing[dest, :, columns] = total.astype(jnp.bfloat16)
+
+    @pl.loop(0, chips - 1)
+    def _(i):
+        for q in range(CHUNKS):
+            far = chips - 1 - i
+
+            @pl.when(far > chip)
+            def _():
+                relay(far, q, has_left, rightward, from_left)
+                rightward(far, q).start()
+
+            @pl.when(i < chip)
+            def _():
+                relay(i, q, has_right, leftward, from_right)
+                leftward(i, q).start()
+
+    for q in range(CHUNKS):
+        for columns in tiles(q):
+            totals[:, columns] = tokens_ref[:, columns].astype(jnp.float32) + partial(chip, columns)
+    for q in range(CHUNKS):
+
+        @pl.when(has_left)
+        def _():
+            rightward(chip, q).wait_recv()
+            for columns in tiles(q):
+                totals[:, columns] += from_left[chip, :, columns].astype(jnp.float32)
+
+        @pl.when(has_right)
+        def _():
+            leftward(chip, q).wait_recv()
+            for columns in tiles(q):
+                totals[:, columns] += from_right[chip, :, columns].astype(jnp.float32)
+
+        for columns in tiles(q):
+            out_ref[:, columns] = totals[:, columns].astype(jnp.bfloat16)
+
+    @pl.loop(0, chips - 1)
+    def _(i):
+        for q in range(CHUNKS):
+            far = chips - 1 - i
+
+            @pl.when(far > chip)
+            def _():
+                rightward(far, q).wait_send()
+
+            @pl.when(i < chip)
+            def _():
+                leftward(i, q).wait_send()
+
+
+def scattered_output(tokens, queries, values, own_weight, other_weight, tensor_count):
+    size, model_width = tokens.shape
+    rows, width = queries.shape
+    chips = tensor_count // 2
+    line = pltpu.VMEM((chips, size, model_width), jnp.bfloat16)
+    flags = pltpu.SemaphoreType.DMA((chips, CHUNKS))
+    return pl.pallas_call(
+        functools.partial(scatter_kernel, tensor_count),
+        out_shape=jax.ShapeDtypeStruct((size, model_width), jnp.bfloat16),
+        in_specs=[pl.BlockSpec(memory_space=pltpu.VMEM)] * 5,
+        out_specs=pl.BlockSpec(memory_space=pltpu.VMEM),
+        scratch_shapes=[
+            pltpu.VMEM((chips, 2, size, width), jnp.bfloat16),
+            pltpu.VMEM((chips, size, width), jnp.bfloat16),
+            line, line, line,
+            pltpu.VMEM((size, model_width), jnp.float32),
+            pltpu.SemaphoreType.DMA,
+            pltpu.SemaphoreType.DMA,
+            flags, flags, flags, flags,
+        ],
+        compiler_params=pltpu.CompilerParams(
+            vmem_limit_bytes=VMEM_LIMIT, collective_id=1, has_side_effects=True
+        ),
+        cost_estimate=pl.CostEstimate(
+            flops=2 * rows * model_width * width, bytes_accessed=4 * model_width * width, transcendentals=0
+        ),
+        name="scattered_output",
+    )(tokens, queries, values, own_weight, other_weight)
 
 
 def short_kernel(seq_count, proj_ref, carried_ref, taps_ref, queries_ref, product_ref):
@@ -399,6 +567,9 @@
 
 def per_device(tokens, norm_gain, in_weight, short_filter, filter_spectrum, out_weight):
     seq_count = lax.axis_size("seq")
+    tensor_count = lax.axis_size("tensor")
+    swap = [(i, i + 1 - 2 * (i % 2)) for i in range(tensor_count)]
+    other_weight = lax.ppermute(out_weight, "tensor", swap)
     inputs = tokens.astype(jnp.float32)
     square_mean = jnp.mean(inputs * inputs, axis=-1, keepdims=True)
     normed = (inputs / jnp.sqrt(square_mean + EPS) * norm_gain).astype(jnp.bfloat16)
@@ -408,7 +579,7 @@
         in_weight.transpose(1, 0, 2),
         filter_spectrum.astype(jnp.bfloat16),
         seq_count,
-        lax.axis_size("tensor"),
+        tensor_count,
     )
     rows = projected.shape[1]
     tables = dft_tables(rows, seq_count)
@@ -419,15 +590,7 @@
     blocks = lax.all_to_all(product, "seq", split_axis=0, concat_axis=0, tiled=True)
     values = long_convolution(blocks, response, tables)
     returned = lax.all_to_all(values, "seq", split_axis=0, concat_axis=0, tiled=True)
-    long_conv = returned.transpose(1, 0, 2).reshape(rows, width).astype(jnp.float32)
-    gated = (queries * long_conv).astype(jnp.bfloat16)
-    summed = lax.psum_scatter(
-        jnp.dot(gated, out_weight, preferred_element_type=jnp.float32).astype(jnp.bfloat16),
-        "tensor",
-        scatter_dimension=0,
-        tiled=True,
-    ).astype(jnp.float32)
-    return (inputs + summed).astype(jnp.bfloat16)
+    return scattered_output(tokens, queries, returned, out_weight, other_weight, tensor_count)
 
 
 def solution(mesh):

time: 277 us -> 248 us (0.90); the launches traced: 272 us -> 248 us
  Pallas kernels: 97.2 us -> 192 us
  waiting for transfers between devices: 97.6 us -> 5.6 us
  between operations: 13.5 us -> 0.06 us
  matrix products: 14.9 us -> 4.31 us
    pallas_call x0 -> x1, Pallas kernels: none -> 94.4 us  [scattered_output(): pl.pallas_call(functools.partial(scatter_kernel, tensor_count), out_shape...]
    reduce_scatter x1 -> x0, waiting for transfers between devices: 93.8 us -> none  [per_device(): lax.psum_scatter(jnp.dot(gated, out_weight, preferred_element_type=jnp.fl...]
    dot_general x1 -> x0, matrix products: 10.6 us -> none  [per_device(): jnp.dot(gated, out_weight, preferred_element_type=jnp.float32)]
    convert_element_type x2 -> x0, local copies, waits for them, and re-layouts: 3.79 us -> none  [per_device(): returned.transpose(1, 0, 2).reshape(rows, width).astype(jnp.float32)]
  transfers between devices with their start and end apart: 3 -> 3, of which waited for: 3 -> 2; matrix products, arithmetic and copies ran while one was open for 4% -> 9% of each run, Pallas kernels for 0% -> 39%
where the time goes in v3:
time: 248 us
  Pallas kernels  192 us (77%)
  blocking collectives  18.9 us (8%)
  other arithmetic  11.9 us (5%)
  local copies, waits for them, and re-layouts  7.78 us (3%)
  starting transfers between devices  7.07 us (3%)
  waiting for transfers between devices  5.6 us (2%)
  matrix products  4.31 us (2%)
    pallas_call x1, Pallas kernels, scattered_output(): pl.pallas_call(functools.partial(scatter_kernel, tensor_count), out_shape...  94.4 us
    pallas_call x1, Pallas kernels, gathered_projection(): pl.pallas_call(functools.partial(gather_kernel, seq_count, tensor_count),...  74.7 us
    all_to_all x1, blocking collectives, per_device(): lax.all_to_all(values, 'seq', split_axis=0, concat_axis=0, tiled=True)  18.9 us
    pallas_call x1, Pallas kernels, long_convolution(): pl.pallas_call(conv_kernel, out_shape=jax.ShapeDtypeStruct((count, rows,...  17.8 us
    convert_element_type x1, other arithmetic, per_device(): filter_spectrum.astype(jnp.bfloat16)  6.02 us
    pallas_call x1, Pallas kernels, short_products(): pl.pallas_call(functools.partial(short_kernel, seq_count), out_shape=(jax...  5.35 us
  transfers between devices with their start and end apart: 3, of which 2 were waited for; matrix products, arithmetic and copies ran while one was open for 9% of the time, Pallas kernels for 39%

profile of v3, /device:TPU:8, one launch (start us, length us, event | category | flops | bytes accessed | tf_op | source)
XLA Modules:
  0.0 247.8 jit_solution(18141238081263266106)
XLA Ops:
  0.0 0.0 collective-permute-start.1
  0.0 1.5 fusion
  1.5 2.5 %fusion.2.normed_ref = bf16[128,4096]{1,0:T(8,128)(2,1)} fusion(bf16[128,4096]{1,0:T(8,128)(2,1)} %tokens_ref.1, f32[4096]{0:T(1024)} %param.13, f32[128]{0:T(128)S(1)} %add_sqrt_fusion), kind=kLoop, calls=%fused_computation.6 | loop fusion | flops 2097152 | bytes 2114048 | tf_op jit(solution)/shard_map/convert_element_type | solution.py:575
  4.1 6.0 %convert_element_type.17.filter_ref = bf16[2,2,512,1024]{3,2,1,0:T(8,128)(2,1)} convert(f32[2,2,512,1024]{3,2,1,0:T(8,128)} %param.16) | non-fusion elementwise | flops 2097152 | bytes 12582912 | tf_op jit(solution)/shard_map/convert_element_type | solution.py:580
  10.1 74.7 %gathered_projection.1 = (bf16[3,1024,512]{2,1,0:T(8,128)(2,1)}, bf16[2,8,128,1024]{3,2,1,0:T(8,128)(2,1)}) custom-call(bf16[128,4096]{1,0:T(8,128)(2,1)} %fusion.2.normed_ref, bf16[3,4096,512]{2,1,0:T(8,128)(2,1)} %bitcast.6, bf16[2,2,512,1024]{3,2,1,0:T(8,128)(2,1)} %convert_element_type.17.filter_ref), custom_call_target="tpu_custom_call" | custom-call | flops 12884901888 | bytes 12582912 | tf_op jit(solution)/shard_map/gathered_projection/pallas_call | solution.py:189
  84.8 0.8 slice.15
  85.6 2.5 %collective-permute-start = (bf16[3,16,512]{2,1,0:T(8,128)(2,1)S(1)}, bf16[3,16,512]{2,1,0:T(8,128)(2,1)S(1)}, u32[]{:S(2)}, u32[]{:S(2)}) collective-permute-start(bf16[3,16,512]{2,1,0:T(8,128)(2,1)S(1)} %slice.15), channel_id=1, source_target_pairs={{0,8},{8,16},{16,24},{1,9},{9,17},{17,25},{2,10},{10,18},{18,26},{... | collective-permute-start | bytes 147464 | tf_op jit(solution)/shard_map/ppermute | solution.py:587
  88.1 1.7 collective-permute-done.carried_ref
  89.8 0.0 copy-start
  89.8 0.6 copy-done
  90.4 5.3 %short_products.1 = (f32[1024,512]{1,0:T(8,128)}, bf16[4,1024,128]{2,1,0:T(8,128)(2,1)}) custom-call(bf16[3,1024,512]{2,1,0:T(8,128)(2,1)} %get-tuple-element.9.proj_ref, bf16[3,16,512]{2,1,0:T(8,128)(2,1)} %copy-done, f32[3,3,512]{2,1,0:T(4,128)} %taps_ref.1), custom_call_target="tpu_custom_call" | custom-call | flops 10485760 | bytes 6291456 | tf_op jit(solution)/shard_map/short_products/pallas_call | solution.py:414
  95.8 4.6 %all-to-all-start = ((bf16[4,1024,128]{2,1,0:T(8,128)(2,1)}), bf16[4,1024,128]{2,1,0:T(8,128)(2,1)}, u32[]{:S(2)}, u32[]{:S(2)}) async-start(bf16[4,1024,128]{2,1,0:T(8,128)(2,1)} %get-tuple-element.11), calls=%async_computation | async-start | bytes 2097152 | tf_op jit(solution)/shard_map/all_to_all | solution.py:590
  100.4 1.3 fusion.3
  101.6 1.5 slice.18
  103.2 0.0 copy-start.1
  103.2 1.3 rev.3
  104.4 0.0 copy-done.1
  104.4 4.3 %add_convert_fusion = bf16[2,3,128,1024]{3,2,1,0:T(8,128)(2,1)S(1)} fusion(bf16[2,3,128,1024]{3,2,1,0:T(8,128)(2,1)} %rev.3, bf16[1024,1024,1,1]{1,0,3,2:T(8,128)(2,1)} %constant.26, f32[2]{0:T(128)S(1)} %copy-done.1, bf16[2,8,128,1024]{3,2,1,0:T(8,128)(2,1)} %get-tuple-element.12), kind=kOutput, calls=%fused_computation | convolution fusion | flops 1613758464 | bytes 6815752 | tf_op jit(solution)/shard_map/ckej,jm->ckem/dot_general | solution.py:544
  108.8 1.8 pad_maximum_fusion.g_ref
  110.6 3.9 %all-to-all-done.x_ref = bf16[4,1024,128]{2,1,0:T(8,128)(2,1)} async-done(((bf16[4,1024,128]{2,1,0:T(8,128)(2,1)}), bf16[4,1024,128]{2,1,0:T(8,128)(2,1)}, u32[]{:S(2)}, u32[]{:S(2)}) %all-to-all-start) | async-done | bytes 1048608 | tf_op jit(solution)/shard_map/all_to_all | solution.py:590
  114.5 17.8 %long_convolution.1 = bf16[4,1024,128]{2,1,0:T(8,128)(2,1)} custom-call(bf16[4,1024,128]{2,1,0:T(8,128)(2,1)} %all-to-all-done.x_ref, bf16[2,5,128,1024]{3,2,1,0:T(8,128)(2,1)} %pad_maximum_fusion.g_ref, bf16[1024,1024]{1,0:T(8,128)(2,1)} %constant.19.clone.cos_ref, bf16[1024,1024]{1,0:T(8,128)(2,1)} %constant.20.clone.sin_ref, ...), custom_call_target="tpu_custom_call" | custom-call | flops 10737418240 | bytes 6815744 | tf_op jit(solution)/shard_map/long_convolution/pallas_call | solution.py:520
  132.3 18.9 %all_to_all.10.values_ref = bf16[4,1024,128]{2,1,0:T(8,128)(2,1)} all-to-all(bf16[4,1024,128]{2,1,0:T(8,128)(2,1)} %long_convolution.1), channel_id=1, replica_groups=mesh['seq'=4,'tensor'=8] {'seq'}, dimensions={0} | all-to-all | bytes 2097152 | tf_op jit(solution)/shard_map/all_to_all | solution.py:592
  151.2 0.0 collective-permute-done.1.other_ref
  151.2 94.4 %scattered_output.1 = bf16[128,4096]{1,0:T(8,128)(2,1)} custom-call(bf16[128,4096]{1,0:T(8,128)(2,1)} %tokens_ref.1, f32[1024,512]{1,0:T(8,128)} %get-tuple-element.10.queries_ref, bf16[4,1024,128]{2,1,0:T(8,128)(2,1)} %all_to_all.10.values_ref, bf16[512,4096]{1,0:T(8,128)(2,1)} %own_ref.1, bf16[512,4096]{1,0:T(8,128)(2,1)} %collective-permute-done.1.other_ref), custom_call_target="tpu_custom_call" | custom-call | flops 4294967296 | bytes 8388608 | tf_op jit(solution)/shard_map/scattered_output/pallas_call | solution.py:366
  245.5 2.3 copy.15
  (1 shorter events, 0.0 us)
Async XLA Ops:
  0.0 151.2 %collective-permute-start.1 = (bf16[512,4096]{1,0:T(8,128)(2,1)}, bf16[512,4096]{1,0:T(8,128)(2,1)}, u32[]{:S(2)}, u32[]{:S(2)}) collective-permute-start(bf16[512,4096]{1,0:T(8,128)(2,1)} %own_ref.1), channel_id=1, source_target_pairs={{0,1},{1,0},{2,3},{3,2},{4,5},{5,4},{6,7},{7,6},{8,9},{9,8},{10,11... | collective-permute-start | bytes 12582920 | tf_op jit(solution)/shard_map/ppermute | solution.py:572
  85.6 4.2 %collective-permute-start = (bf16[3,16,512]{2,1,0:T(8,128)(2,1)S(1)}, bf16[3,16,512]{2,1,0:T(8,128)(2,1)S(1)}, u32[]{:S(2)}, u32[]{:S(2)}) collective-permute-start(bf16[3,16,512]{2,1,0:T(8,128)(2,1)S(1)} %slice.15), channel_id=1, source_target_pairs={{0,8},{8,16},{16,24},{1,9},{9,17},{17,25},{2,10},{10,18},{18,26},{... | collective-permute-start | bytes 147464 | tf_op jit(solution)/shard_map/ppermute | solution.py:587
  89.8 0.6 copy-start
  95.8 18.7 %all-to-all-start = ((bf16[4,1024,128]{2,1,0:T(8,128)(2,1)}), bf16[4,1024,128]{2,1,0:T(8,128)(2,1)}, u32[]{:S(2)}, u32[]{:S(2)}) async-start(bf16[4,1024,128]{2,1,0:T(8,128)(2,1)} %get-tuple-element.11), calls=%async_computation | async-start | bytes 2097152 | tf_op jit(solution)/shard_map/all_to_all | solution.py:590
  103.2 1.3 copy-start.1

commit v4 on v3

--- a/solution.py
+++ b/solution.py
@@ -90,21 +90,19 @@
             device_id_type=MESH,
         )
 
-    def multiply(other):
-        for q in range(CHUNKS):
-            passed(other * 2 + 1 - core, q, sibling, to_sibling).wait_recv()
+    def multiply(other, j):
+        if j == 0:
+            for q in range(CHUNKS):
+                passed(other * 2 + 1 - core, q, sibling, to_sibling).wait_recv()
         rows = pl.ds(pl.multiple_of(other * 2 * size, 2 * size), 2 * size)
-
-        @pl.loop(0, 3)
-        def _(j):
-            for begin in range(0, width, 256):
-                columns = min(256, width - begin)
-                value = jnp.dot(
-                    held[pl.ds(other * 2, 2)].reshape(2 * size, held.shape[2]),
-                    weights[j, :, pl.ds(begin, columns)],
-                    preferred_element_type=jnp.float32,
-                )
-                proj_ref[j, rows, pl.ds(begin, columns)] = value.astype(jnp.bfloat16)
+        for begin in range(0, width, 256):
+            columns = min(256, width - begin)
+            value = jnp.dot(
+                held[pl.ds(other * 2, 2)].reshape(2 * size, held.shape[2]),
+                weights[j, :, pl.ds(begin, columns)],
+                preferred_element_type=jnp.float32,
+            )
+            proj_ref[j, rows, pl.ds(begin, columns)] = value.astype(jnp.bfloat16)
 
     for q in range(CHUNKS):
 
@@ -120,7 +118,6 @@
     for k in range(1, seq_count):
         filter_copy(k).start()
     weight_copy.wait()
-    multiply(chip)
 
     def sides(distance):
         yield chip + distance, chip + distance < chips, right, has_left, left, to_left
@@ -142,11 +139,19 @@
 
                     passed(block, q, sibling, to_sibling).start()
 
-        for other, exists, *_rest in sides(distance):
-
-            @pl.when(exists)
-            def _():
-                multiply(other)
+            if q < 3:
+                for side, (other, exists, *_rest) in enumerate(sides(distance - 1)):
+
+                    @pl.when(exists & (distance > side))
+                    def _():
+                        multiply(other, q)
+
+    for other, exists, *_rest in sides(chips - 1):
+
+        @pl.when(exists)
+        def _():
+            for j in range(3):
+                multiply(other, j)
 
     for q in range(CHUNKS):
 

time: 248 us -> 248 us (level)
  transfers between devices with their start and end apart: 3 -> 3, of which waited for: 2 -> 2; matrix products, arithmetic and copies ran while one was open for 9% -> 9% of each run, Pallas kernels for 39% -> 40%
where the time goes in v4:
time: 248 us; the launch traced here: 247 us
  Pallas kernels  192 us (77%)
  blocking collectives  18.9 us (8%)
  other arithmetic  11.9 us (5%)
  local copies, waits for them, and re-layouts  7.78 us (3%)
  starting transfers between devices  7.25 us (3%)
  waiting for transfers between devices  5.24 us (2%)
  matrix products  4.31 us (2%)
    pallas_call x1, Pallas kernels, scattered_output(): pl.pallas_call(functools.partial(scatter_kernel, tensor_count), out_shape...  94 us
    pallas_call x1, Pallas kernels, gathered_projection(): pl.pallas_call(functools.partial(gather_kernel, seq_count, tensor_count),...  74.7 us
    all_to_all x1, blocking collectives, per_device(): lax.all_to_all(values, 'seq', split_axis=0, concat_axis=0, tiled=True)  18.9 us
    pallas_call x1, Pallas kernels, long_convolution(): pl.pallas_call(conv_kernel, out_shape=jax.ShapeDtypeStruct((count, rows,...  17.8 us
    convert_element_type x1, other arithmetic, per_device(): filter_spectrum.astype(jnp.bfloat16)  6.02 us
    pallas_call x1, Pallas kernels, short_products(): pl.pallas_call(functools.partial(short_kernel, seq_count), out_shape=(jax...  5.35 us
  transfers between devices with their start and end apart: 3, of which 2 were waited for; matrix products, arithmetic and copies ran while one was open for 9% of the time, Pallas kernels for 40%

profile of v4, /device:TPU:8, one launch (start us, length us, event | category | flops | bytes accessed | tf_op | source)
XLA Modules:
  0.0 247.3 jit_solution(1691253382575108343)
XLA Ops:
  0.0 0.0 collective-permute-start.1
  0.0 1.5 fusion
  1.5 2.5 %fusion.2.normed_ref = bf16[128,4096]{1,0:T(8,128)(2,1)} fusion(bf16[128,4096]{1,0:T(8,128)(2,1)} %tokens_ref.1, f32[4096]{0:T(1024)} %param.13, f32[128]{0:T(128)S(1)} %add_sqrt_fusion), kind=kLoop, calls=%fused_computation.6 | loop fusion | flops 2097152 | bytes 2114048 | tf_op jit(solution)/shard_map/convert_element_type | solution.py:580
  4.1 6.0 %convert_element_type.17.filter_ref = bf16[2,2,512,1024]{3,2,1,0:T(8,128)(2,1)} convert(f32[2,2,512,1024]{3,2,1,0:T(8,128)} %param.16) | non-fusion elementwise | flops 2097152 | bytes 12582912 | tf_op jit(solution)/shard_map/convert_element_type | solution.py:585
  10.1 74.7 %gathered_projection.1 = (bf16[3,1024,512]{2,1,0:T(8,128)(2,1)}, bf16[2,8,128,1024]{3,2,1,0:T(8,128)(2,1)}) custom-call(bf16[128,4096]{1,0:T(8,128)(2,1)} %fusion.2.normed_ref, bf16[3,4096,512]{2,1,0:T(8,128)(2,1)} %bitcast.6, bf16[2,2,512,1024]{3,2,1,0:T(8,128)(2,1)} %convert_element_type.17.filter_ref), custom_call_target="tpu_custom_call" | custom-call | flops 12884901888 | bytes 12582912 | tf_op jit(solution)/shard_map/gathered_projection/pallas_call | solution.py:194
  84.8 0.8 slice.15
  85.6 2.7 %collective-permute-start = (bf16[3,16,512]{2,1,0:T(8,128)(2,1)S(1)}, bf16[3,16,512]{2,1,0:T(8,128)(2,1)S(1)}, u32[]{:S(2)}, u32[]{:S(2)}) collective-permute-start(bf16[3,16,512]{2,1,0:T(8,128)(2,1)S(1)} %slice.15), channel_id=1, source_target_pairs={{0,8},{8,16},{16,24},{1,9},{9,17},{17,25},{2,10},{10,18},{18,26},{... | collective-permute-start | bytes 147464 | tf_op jit(solution)/shard_map/ppermute | solution.py:592
  88.3 1.6 collective-permute-done.carried_ref
  89.8 0.0 copy-start
  89.8 0.6 copy-done
  90.4 5.3 %short_products.1 = (f32[1024,512]{1,0:T(8,128)}, bf16[4,1024,128]{2,1,0:T(8,128)(2,1)}) custom-call(bf16[3,1024,512]{2,1,0:T(8,128)(2,1)} %get-tuple-element.9.proj_ref, bf16[3,16,512]{2,1,0:T(8,128)(2,1)} %copy-done, f32[3,3,512]{2,1,0:T(4,128)} %taps_ref.1), custom_call_target="tpu_custom_call" | custom-call | flops 10485760 | bytes 6291456 | tf_op jit(solution)/shard_map/short_products/pallas_call | solution.py:419
  95.8 4.6 %all-to-all-start = ((bf16[4,1024,128]{2,1,0:T(8,128)(2,1)}), bf16[4,1024,128]{2,1,0:T(8,128)(2,1)}, u32[]{:S(2)}, u32[]{:S(2)}) async-start(bf16[4,1024,128]{2,1,0:T(8,128)(2,1)} %get-tuple-element.11), calls=%async_computation | async-start | bytes 2097152 | tf_op jit(solution)/shard_map/all_to_all | solution.py:595
  100.4 1.3 fusion.3
  101.6 1.5 slice.18
  103.2 0.0 copy-start.1
  103.2 1.3 rev.3
  104.4 0.0 copy-done.1
  104.4 4.3 %add_convert_fusion = bf16[2,3,128,1024]{3,2,1,0:T(8,128)(2,1)S(1)} fusion(bf16[2,3,128,1024]{3,2,1,0:T(8,128)(2,1)} %rev.3, bf16[1024,1024,1,1]{1,0,3,2:T(8,128)(2,1)} %constant.26, f32[2]{0:T(128)S(1)} %copy-done.1, bf16[2,8,128,1024]{3,2,1,0:T(8,128)(2,1)} %get-tuple-element.12), kind=kOutput, calls=%fused_computation | convolution fusion | flops 1613758464 | bytes 6815752 | tf_op jit(solution)/shard_map/ckej,jm->ckem/dot_general | solution.py:549
  108.8 1.8 pad_maximum_fusion.g_ref
  110.6 3.7 %all-to-all-done.x_ref = bf16[4,1024,128]{2,1,0:T(8,128)(2,1)} async-done(((bf16[4,1024,128]{2,1,0:T(8,128)(2,1)}), bf16[4,1024,128]{2,1,0:T(8,128)(2,1)}, u32[]{:S(2)}, u32[]{:S(2)}) %all-to-all-start) | async-done | bytes 1048608 | tf_op jit(solution)/shard_map/all_to_all | solution.py:595
  114.3 17.8 %long_convolution.1 = bf16[4,1024,128]{2,1,0:T(8,128)(2,1)} custom-call(bf16[4,1024,128]{2,1,0:T(8,128)(2,1)} %all-to-all-done.x_ref, bf16[2,5,128,1024]{3,2,1,0:T(8,128)(2,1)} %pad_maximum_fusion.g_ref, bf16[1024,1024]{1,0:T(8,128)(2,1)} %constant.19.clone.cos_ref, bf16[1024,1024]{1,0:T(8,128)(2,1)} %constant.20.clone.sin_ref, ...), custom_call_target="tpu_custom_call" | custom-call | flops 10737418240 | bytes 6815744 | tf_op jit(solution)/shard_map/long_convolution/pallas_call | solution.py:525
  132.1 18.9 %all_to_all.10.values_ref = bf16[4,1024,128]{2,1,0:T(8,128)(2,1)} all-to-all(bf16[4,1024,128]{2,1,0:T(8,128)(2,1)} %long_convolution.1), channel_id=1, replica_groups=mesh['seq'=4,'tensor'=8] {'seq'}, dimensions={0} | all-to-all | bytes 2097152 | tf_op jit(solution)/shard_map/all_to_all | solution.py:597
  151.0 0.0 collective-permute-done.1.other_ref
  151.0 94.0 %scattered_output.1 = bf16[128,4096]{1,0:T(8,128)(2,1)} custom-call(bf16[128,4096]{1,0:T(8,128)(2,1)} %tokens_ref.1, f32[1024,512]{1,0:T(8,128)} %get-tuple-element.10.queries_ref, bf16[4,1024,128]{2,1,0:T(8,128)(2,1)} %all_to_all.10.values_ref, bf16[512,4096]{1,0:T(8,128)(2,1)} %own_ref.1, bf16[512,4096]{1,0:T(8,128)(2,1)} %collective-permute-done.1.other_ref), custom_call_target="tpu_custom_call" | custom-call | flops 4294967296 | bytes 8388608 | tf_op jit(solution)/shard_map/scattered_output/pallas_call | solution.py:371
  245.0 2.3 copy.15
  (1 shorter events, 0.0 us)
Async XLA Ops:
  0.0 151.0 %collective-permute-start.1 = (bf16[512,4096]{1,0:T(8,128)(2,1)}, bf16[512,4096]{1,0:T(8,128)(2,1)}, u32[]{:S(2)}, u32[]{:S(2)}) collective-permute-start(bf16[512,4096]{1,0:T(8,128)(2,1)} %own_ref.1), channel_id=1, source_target_pairs={{0,1},{1,0},{2,3},{3,2},{4,5},{5,4},{6,7},{7,6},{8,9},{9,8},{10,11... | collective-permute-start | bytes 12582920 | tf_op jit(solution)/shard_map/ppermute | solution.py:577
  85.6 4.2 %collective-permute-start = (bf16[3,16,512]{2,1,0:T(8,128)(2,1)S(1)}, bf16[3,16,512]{2,1,0:T(8,128)(2,1)S(1)}, u32[]{:S(2)}, u32[]{:S(2)}) collective-permute-start(bf16[3,16,512]{2,1,0:T(8,128)(2,1)S(1)} %slice.15), channel_id=1, source_target_pairs={{0,8},{8,16},{16,24},{1,9},{9,17},{17,25},{2,10},{10,18},{18,26},{... | collective-permute-start | bytes 147464 | tf_op jit(solution)/shard_map/ppermute | solution.py:592
  89.8 0.6 copy-start
  95.8 18.5 %all-to-all-start = ((bf16[4,1024,128]{2,1,0:T(8,128)(2,1)}), bf16[4,1024,128]{2,1,0:T(8,128)(2,1)}, u32[]{:S(2)}, u32[]{:S(2)}) async-start(bf16[4,1024,128]{2,1,0:T(8,128)(2,1)} %get-tuple-element.11), calls=%async_computation | async-start | bytes 2097152 | tf_op jit(solution)/shard_map/all_to_all | solution.py:595
  103.2 1.3 copy-start.1
